TPU v7x, 32 devices: a whole 2x2x4 slice. The times are simulated.
32 devices in a mesh: gx: 2 (over x), gy: 4 (over y, core), tx: 4 (over z).
Axes of the slice: x: 2, y: 2, z: 4, core: 2. Of those that a mesh axis runs over, the one named last changes fastest.
Arguments:
- src_cell: int32 [8], P('tx'), may hold values from 0 to 65535
- basis: bfloat16 [16, 2, 3, 8, 16, 512], P('tx', None, None, None, 'gx', 'gy'), as said below
- images: bfloat16 [16, 2, 3, 8, 16, 512], P('tx', None, None, None, 'gx', 'gy'), as said below
- induction: bfloat16 [3, 8, 16, 512], P(None, 'tx', 'gx', 'gy'), may hold values from 0.25 to 4
Outputs:
- solution: float32 [8, 2, 3, 8, 16, 512], P('tx', None, None, None, 'gx', 'gy')
- residual: float32 [8, 2, 3, 8, 16, 512], P('tx', None, None, None, 'gx', 'gy')
Inputs may be any that keep to these rules, and one draw needn't show every extreme that they name: `basis`: entries of order one. `images`: entries of order one.
All inputs are finite; a program needn't handle non-finite values.
Results may differ from a plain program's by a relative error of at most 0.0003.
Values may be sent and summed in bfloat16 or wider, within the bound.
A program may use at most 64 MiB of HBM per device.

v0:
```python
import jax
import jax.numpy as jnp
from jax import lax
from jax.sharding import PartitionSpec as P

CYCLES = 2
ARNOLDI = 2


eps = 1e-06


def with_halo(x, sides, width):
    for axis, dim in sides:
        size, length = (lax.axis_size(axis), x.shape[dim])
        up = [(i, (i + 1) % size) for i in range(size - 1)]
        down = [(j, i) for i, j in up]
        last = lax.slice_in_dim(x, length - width, length, axis=dim)
        initial = lax.slice_in_dim(x, 0, width, axis=dim)
        before = lax.ppermute(last, axis, up)
        after = lax.ppermute(initial, axis, down)
        x = jnp.concatenate([before, x, after], axis=dim)
    return x


def differ(field, axis, forward):
    axis = field.ndim + axis
    count = field.shape[axis]
    delta = lax.slice_in_dim(field, 1, count, axis=axis) - lax.slice_in_dim(
        field, 0, count - 1, axis=axis
    )
    zero = jnp.zeros_like(lax.slice_in_dim(field, 0, 1, axis=axis))
    if forward:
        return jnp.concatenate([delta, zero], axis=axis)
    return jnp.concatenate([zero, delta], axis=axis)


def curl_curl(padded):
    e_x = padded[..., 0, :, :, :]
    e_y = padded[..., 1, :, :, :]
    e_z = padded[..., 2, :, :, :]
    b_x = differ(e_z, -1, True) - differ(e_y, -3, True)
    b_y = differ(e_x, -3, True) - differ(e_z, -2, True)
    b_z = differ(e_y, -2, True) - differ(e_x, -1, True)
    c_x = differ(b_z, -1, False) - differ(b_y, -3, False)
    c_y = differ(b_x, -3, False) - differ(b_z, -2, False)
    c_z = differ(b_y, -2, False) - differ(b_x, -1, False)
    whole = jnp.stack([c_x, c_y, c_z], axis=-4)
    return whole[..., 1:-1, 1:-1, 1:-1]


def apply_operator(field, induct):
    framed = with_halo(field, (("gx", 4), ("gy", 5)), 1)
    padded = jnp.pad(framed, [(0, 0), (0, 0), (0, 0), (1, 1), (0, 0), (0, 0)])
    curled = curl_curl(padded)
    real_part = curled[:, 0] - induct[None] * field[:, 1]
    imag_part = curled[:, 1] + induct[None] * field[:, 0]
    return jnp.stack([real_part, imag_part], axis=1)


def source_field(cells, z_pos, x_pos, y_pos, size_x, size_y, induct):
    plane = size_x * size_y
    src_z = cells // plane
    rest = cells % plane
    src_x = rest // size_y
    src_y = rest % size_y
    d_z = (z_pos[None, :] - src_z[:, None]).astype(jnp.float32)
    d_x = (x_pos[None, :] - src_x[:, None]).astype(jnp.float32)
    d_y = (y_pos[None, :] - src_y[:, None]).astype(jnp.float32)
    dist = jnp.sqrt(
        d_z[:, :, None, None] ** 2 + d_x[:, None, :, None] ** 2 + d_y[:, None, None, :] ** 2
    )
    primary = jnp.exp(-dist / ((size_x + size_y) / 8.0))
    weights = jnp.array([1.0, 0.5, 0.25], dtype=jnp.float32)
    real_part = (induct - 1.0)[None] * weights[None, :, None, None, None] * primary[:, None]
    return jnp.stack([real_part, 0.5 * real_part], axis=1)


def inner_basis(vectors, field):
    return jnp.einsum(
        "kpczxy,spczxy->ks",
        vectors,
        field,
        precision=lax.Precision.HIGHEST,
        preferred_element_type=jnp.float32,
    )


def combine(coeffs, vectors):
    return jnp.einsum(
        "ks,kpczxy->spczxy",
        coeffs,
        vectors,
        precision=lax.Precision.HIGHEST,
        preferred_element_type=jnp.float32,
    )


def per_source(left, right):
    return jnp.sum(left * right, axis=(1, 2, 3, 4, 5))


def expand(values):
    return values[:, None, None, None, None, None]


def small_solve(matrix, rhs):
    factor = jnp.linalg.cholesky(matrix)
    return jax.scipy.linalg.cho_solve((factor, True), rhs)


def on_device(src_cell, basis, images, induction):
    all_basis, all_images, gathered = (
        lax.all_gather(basis, "tx", axis=0, tiled=True),
        lax.all_gather(images, "tx", axis=0, tiled=True),
        lax.all_gather(induction, "tx", axis=1, tiled=True),
    )
    induct = gathered.astype(jnp.float32)
    depth = basis.shape[3]
    width_x = basis.shape[4]
    width_y = basis.shape[5]
    size_x = width_x * lax.axis_size("gx")
    size_y = width_y * lax.axis_size("gy")
    z_pos = jnp.arange(depth, dtype=jnp.int32)
    x_pos = lax.axis_index("gx") * width_x + jnp.arange(width_x, dtype=jnp.int32)
    y_pos = lax.axis_index("gy") * width_y + jnp.arange(width_y, dtype=jnp.int32)
    rhs = source_field(src_cell, z_pos, x_pos, y_pos, size_x, size_y, induct)
    gram_part = jnp.einsum(
        "kpczxy,lpczxy->kl", all_images, all_images, preferred_element_type=jnp.float32
    )
    gram, start_inner = lax.psum((gram_part, inner_basis(all_images, rhs)), ("gx", "gy"))
    factor = jnp.linalg.cholesky(gram)
    h_zero = jax.scipy.linalg.cho_solve((factor, True), start_inner)
    residual = rhs - combine(h_zero, all_images)
    solution = combine(h_zero, all_basis)
    for cycle in range(CYCLES):
        beta = jnp.sqrt(lax.psum(per_source(residual, residual), ("gx", "gy")) + eps)
        krylov = [residual / expand(beta)]
        h_cols = []
        g_cols = []
        for step in range(ARNOLDI):
            work = apply_operator(krylov[step], induct)
            g_raw = lax.psum(inner_basis(all_images, work), ("gx", "gy"))
            g_now = jax.scipy.linalg.cho_solve((factor, True), g_raw)
            work = work - combine(g_now, all_images)
            h_now = lax.psum(jnp.stack([per_source(vec, work) for vec in krylov]), ("gx", "gy"))
            for index in range(step + 1):
                work = work - expand(h_now[index]) * krylov[index]
            h_next = jnp.sqrt(lax.psum(per_source(work, work), ("gx", "gy")) + eps)
            krylov.append(work / expand(h_next))
            pad_rows = jnp.zeros((ARNOLDI - step - 1, h_next.shape[0]), dtype=jnp.float32)
            h_cols.append(jnp.concatenate([h_now, h_next[None], pad_rows], axis=0))
            g_cols.append(g_now)
        hess = jnp.stack(h_cols, axis=1)
        g_all = jnp.stack(g_cols, axis=1)
        normal = jnp.einsum("ijs,iks->sjk", hess, hess, precision=lax.Precision.HIGHEST)
        target = beta[:, None] * jnp.transpose(hess[0])
        y_coef = jax.vmap(small_solve)(normal, target)
        update = expand(y_coef[:, 0]) * krylov[0]
        step = 1
        update = update + expand(y_coef[:, step]) * krylov[step]
        u_coef = jnp.einsum("kjs,sj->ks", g_all, y_coef, precision=lax.Precision.HIGHEST)
        solution = solution + update - combine(u_coef, all_basis)
        first = jnp.zeros((ARNOLDI + 1, beta.shape[0]), dtype=jnp.float32).at[0].set(beta)
        t_coef = first - jnp.einsum("ijs,sj->is", hess, y_coef, precision=lax.Precision.HIGHEST)
        residual = expand(t_coef[0]) * krylov[0]
        for index in range(1, ARNOLDI + 1):
            residual = residual + expand(t_coef[index]) * krylov[index]
    return (solution, residual)


def solution(mesh):
    in_specs = (
        P("tx"),
        P("tx", None, None, None, "gx", "gy"),
        P("tx", None, None, None, "gx", "gy"),
        P(None, "tx", "gx", "gy"),
    )
    out_specs = (P("tx", None, None, None, "gx", "gy"), P("tx", None, None, None, "gx", "gy"))
    return jax.shard_map(
        on_device, mesh=mesh, in_specs=in_specs, out_specs=out_specs, check_vma=False
    )
```

profile of v0, /device:TPU:0, one launch (start us, length us, event | category | flops | bytes accessed | tf_op | source)
XLA Modules:
  0.0 435.0 jit_solution(8338258876400657625)
XLA Ops:
  7.9 15.0 %all_gather.10 = bf16[3,8,8,128]{3,2,1,0:T(8,128)(2,1)S(1)} all-gather(bf16[3,2,8,128]{3,2,1,0:T(8,128)(2,1)} %param.17), channel_id=1, replica_groups=mesh['gx'=2,'gy'=4,'tx'=4] {'tx'}, dimensions={1}, use_global_device_ids=true | all-gather | bytes 61440 | tf_op jit(solution)/shard_map/all_gather | solution.py:116
  24.9 24.5 %all-gather.3.cloned.1.call-done = bf16[16,2,3,8,8,128]{5,4,3,2,1,0:T(8,128)(2,1)} async-done(((bf16[4,2,3,8,8,128]{5,4,3,2,1,0:T(8,128)(2,1)}), bf16[16,2,3,8,8,128]{5,4,3,2,1,0:T(8,128)(2,1)}) %all-gather.3.cloned.1.call-update) | async-done | bytes 1572880 | tf_op jit(solution)/shard_map/all_gather | solution.py:115
  49.4 5.4 %convolution_bitcast_fusion = f32[16,16]{0,1:T(8,128)S(1)} fusion(bf16[16,2,3,8,8,128]{5,4,3,2,1,0:T(8,128)(2,1)} %all-gather.3.cloned.1.call-done), kind=kOutput, calls=%fused_computation.29 | convolution fusion | flops 25165824 | bytes 1573888 | tf_op jit(solution)/shard_map/kpczxy,lpczxy->kl/dot_general | solution.py:128
  54.8 3.7 convolution_bitcast_fusion.8
  58.4 14.0 %all-reduce.54 = (f32[16,2]{0,1:T(2,128)S(1)}, f32[16,16]{0,1:T(8,128)S(1)}) all-reduce(f32[16,2]{0,1:T(2,128)S(1)} %convolution_bitcast_fusion.8, f32[16,16]{0,1:T(8,128)S(1)} %convolution_bitcast_fusion), channel_id=1, replica_groups=mesh['gx'=2,'gy'=4,'tx'=4] {'gx','gy'}, use_global_device_ids=true, to_apply=%region_3.4 | all-reduce | flops 288 | bytes 2304 | tf_op jit(solution)/shard_map/psum | solution.py:131
  72.5 1.5 cholesky.32
  75.3 1.2 custom-call.22
  76.8 3.3 multiply_reduce_fusion.11
  80.1 11.8 %psum.114 = f32[2]{0:T(128)S(1)} all-reduce(f32[2]{0:T(128)S(1)} %get-tuple-element.119), channel_id=1, replica_groups=mesh['gx'=2,'gy'=4,'tx'=4] {'gx','gy'}, use_global_device_ids=true, to_apply=%region_5.7 | all-reduce | flops 2 | bytes 16 | tf_op jit(solution)/shard_map/psum | solution.py:137
  92.1 2.5 collective-permute-start
  94.6 1.3 collective-permute-start.1
  96.3 4.3 collective-permute-done.1
  101.4 1.3 collective-permute-start.2
  102.7 1.5 collective-permute-start.3
  104.3 2.2 collective-permute-done.3
  106.5 2.4 select_maximum_fusion.12
  116.5 3.7 convolution_bitcast_fusion.7
  120.2 29.2 %psum.115 = f32[16,2]{0,1:T(2,128)S(1)} all-reduce(f32[16,2]{0,1:T(2,128)S(1)} %convolution_bitcast_fusion.7), channel_id=1, replica_groups=mesh['gx'=2,'gy'=4,'tx'=4] {'gx','gy'}, use_global_device_ids=true, to_apply=%region_6.8 | all-reduce | flops 32 | bytes 256 | tf_op jit(solution)/shard_map/psum | solution.py:143
  149.7 3.3 multiply_reduce_fusion.10
  153.0 11.8 %psum.116 = f32[1,2]{1,0:T(1,128)S(1)} all-reduce(f32[1,2]{1,0:T(1,128)S(1)} %bitcast.337), channel_id=1, replica_groups=mesh['gx'=2,'gy'=4,'tx'=4] {'gx','gy'}, use_global_device_ids=true, to_apply=%region_8.10 | all-reduce | flops 2 | bytes 16 | tf_op jit(solution)/shard_map/psum | solution.py:146
  165.4 11.8 %psum.117 = f32[2]{0:T(128)S(1)} all-reduce(f32[2]{0:T(128)S(1)} %get-tuple-element.49), channel_id=1, replica_groups=mesh['gx'=2,'gy'=4,'tx'=4] {'gx','gy'}, use_global_device_ids=true, to_apply=%region_10.12 | all-reduce | flops 2 | bytes 16 | tf_op jit(solution)/shard_map/psum | solution.py:149
  177.5 1.8 collective-permute-start.4
  179.3 1.3 collective-permute-start.5
  181.0 4.3 collective-permute-done.5
  186.1 1.3 collective-permute-start.6
  187.4 1.3 collective-permute-start.7
  188.9 2.4 collective-permute-done.7
  191.3 2.4 select_maximum_fusion.8
  201.3 3.6 convolution_bitcast_fusion.6
  204.9 18.9 %psum.118 = f32[16,2]{0,1:T(2,128)S(1)} all-reduce(f32[16,2]{0,1:T(2,128)S(1)} %convolution_bitcast_fusion.6), channel_id=1, replica_groups=mesh['gx'=2,'gy'=4,'tx'=4] {'gx','gy'}, use_global_device_ids=true, to_apply=%region_11.13 | all-reduce | flops 32 | bytes 256 | tf_op jit(solution)/shard_map/psum | solution.py:143
  224.1 3.4 multiply_reduce_fusion.8
  227.6 11.8 %psum.119 = f32[2,2]{1,0:T(2,128)S(1)} all-reduce(f32[2,2]{1,0:T(2,128)S(1)} %pad_maximum_fusion.26), channel_id=1, replica_groups=mesh['gx'=2,'gy'=4,'tx'=4] {'gx','gy'}, use_global_device_ids=true, to_apply=%region_14.16 | all-reduce | flops 4 | bytes 32 | tf_op jit(solution)/shard_map/psum | solution.py:146
  240.1 11.8 %psum.120 = f32[2]{0:T(128)S(1)} all-reduce(f32[2]{0:T(128)S(1)} %get-tuple-element.47), channel_id=1, replica_groups=mesh['gx'=2,'gy'=4,'tx'=4] {'gx','gy'}, use_global_device_ids=true, to_apply=%region_16.18 | all-reduce | flops 2 | bytes 16 | tf_op jit(solution)/shard_map/psum | solution.py:149
  254.9 11.8 %psum.121 = f32[2]{0:T(128)S(1)} all-reduce(f32[2]{0:T(128)S(1)} %get-tuple-element.45), channel_id=1, replica_groups=mesh['gx'=2,'gy'=4,'tx'=4] {'gx','gy'}, use_global_device_ids=true, to_apply=%region_20.24 | all-reduce | flops 2 | bytes 16 | tf_op jit(solution)/shard_map/psum | solution.py:137
  267.0 1.9 collective-permute-start.8
  268.9 1.3 collective-permute-start.9
  270.2 3.7 convolution_add_fusion
  275.7 1.3 collective-permute-start.10
  277.0 1.7 collective-permute-start.11
  278.8 2.0 collective-permute-done.11
  280.9 2.4 select_maximum_fusion.4
  287.3 0.9 fusion.5
  290.9 3.7 convolution_bitcast_fusion.5
  294.5 18.9 %psum.122 = f32[16,2]{0,1:T(2,128)S(1)} all-reduce(f32[16,2]{0,1:T(2,128)S(1)} %convolution_bitcast_fusion.5), channel_id=1, replica_groups=mesh['gx'=2,'gy'=4,'tx'=4] {'gx','gy'}, use_global_device_ids=true, to_apply=%region_21.25 | all-reduce | flops 32 | bytes 256 | tf_op jit(solution)/shard_map/psum | solution.py:143
  313.7 3.3 multiply_reduce_fusion.4
  317.0 11.8 %psum.123 = f32[1,2]{1,0:T(1,128)S(1)} all-reduce(f32[1,2]{1,0:T(1,128)S(1)} %bitcast.338), channel_id=1, replica_groups=mesh['gx'=2,'gy'=4,'tx'=4] {'gx','gy'}, use_global_device_ids=true, to_apply=%region_23.27 | all-reduce | flops 2 | bytes 16 | tf_op jit(solution)/shard_map/psum | solution.py:146
  329.4 11.8 %psum.124 = f32[2]{0:T(128)S(1)} all-reduce(f32[2]{0:T(128)S(1)} %get-tuple-element.43), channel_id=1, replica_groups=mesh['gx'=2,'gy'=4,'tx'=4] {'gx','gy'}, use_global_device_ids=true, to_apply=%region_25.29 | all-reduce | flops 2 | bytes 16 | tf_op jit(solution)/shard_map/psum | solution.py:149
  341.4 3.7 collective-permute-start.12
  345.1 1.3 collective-permute-start.13
  346.8 4.3 collective-permute-done.13
  351.9 1.3 collective-permute-start.14
  353.2 1.3 collective-permute-start.15
  354.7 2.3 collective-permute-done.15
  357.0 2.4 select_maximum_fusion
  363.4 0.9 fusion.4
  367.0 3.7 convolution_bitcast_fusion.4
  370.7 18.8 %psum.125 = f32[16,2]{0,1:T(2,128)S(1)} all-reduce(f32[16,2]{0,1:T(2,128)S(1)} %convolution_bitcast_fusion.4), channel_id=1, replica_groups=mesh['gx'=2,'gy'=4,'tx'=4] {'gx','gy'}, use_global_device_ids=true, to_apply=%region_26.30 | all-reduce | flops 32 | bytes 256 | tf_op jit(solution)/shard_map/psum | solution.py:143
  389.7 3.4 multiply_reduce_fusion.2
  393.2 11.8 %psum.126 = f32[2,2]{1,0:T(2,128)S(1)} all-reduce(f32[2,2]{1,0:T(2,128)S(1)} %pad_maximum_fusion.27), channel_id=1, replica_groups=mesh['gx'=2,'gy'=4,'tx'=4] {'gx','gy'}, use_global_device_ids=true, to_apply=%region_29.33 | all-reduce | flops 4 | bytes 32 | tf_op jit(solution)/shard_map/psum | solution.py:146
  405.0 1.4 multiply_reduce_fusion
  406.4 11.8 %psum.127 = f32[2]{0:T(128)S(1)} all-reduce(f32[2]{0:T(128)S(1)} %get-tuple-element.41), channel_id=1, replica_groups=mesh['gx'=2,'gy'=4,'tx'=4] {'gx','gy'}, use_global_device_ids=true, to_apply=%region_31.35 | all-reduce | flops 2 | bytes 16 | tf_op jit(solution)/shard_map/psum | solution.py:149
  420.3 1.5 multiply_add_fusion
  422.9 2.7 fusion
  425.6 1.5 convolution_subtract_fusion
  (209 shorter events, 49.6 us)
Async XLA Ops:
  7.2 42.2 %all-gather.3.cloned.1.call-start = ((), (), s32[]{:S(2)}) async-start(), calls=%async_computation | async-start | bytes 1966080 | tf_op jit(solution)/shard_map/all_gather | solution.py:115
  7.9 262.3 %all-gather.5.cloned.1.call-start = ((), (), s32[]{:S(2)}) async-start(), calls=%async_computation.1 | async-start | bytes 1966080 | tf_op jit(solution)/shard_map/all_gather | solution.py:114
  49.4 5.4 %copy-start.1 = (bf16[16,2,3,8,8,128]{5,4,3,2,1,0:T(8,128)(2,1)S(1)}, bf16[16,2,3,8,8,128]{5,4,3,2,1,0:T(8,128)(2,1)}, u32[]{:S(2)}) copy-start(bf16[16,2,3,8,8,128]{5,4,3,2,1,0:T(8,128)(2,1)} %all-gather.3.cloned.1.call-done) | copy-start | bytes 4718596
  92.1 4.2 collective-permute-start
  94.6 6.0 %collective-permute-start.1 = (f32[2,2,3,8,1,128]{5,0,3,4,1,2:T(2,128)S(1)}, f32[2,2,3,8,1,128]{5,0,3,4,1,2:T(2,128)S(1)}, u32[]{:S(2)}, u32[]{:S(2)}) collective-permute-start(f32[2,2,3,8,1,128]{5,0,3,4,1,2:T(2,128)S(1)} %get-tuple-element.90), channel_id=1, source_target_pairs={{16,0},{17,1},{18,2},{19,3},{20,4},{21,5},{22,6},{23,7},{24,8},{25... | collective-permute-start | bytes 147464 | tf_op jit(solution)/shard_map/ppermute | solution.py:21
  101.4 2.9 collective-permute-start.2
  102.7 3.8 collective-permute-start.3
  115.1 1.4 copy-start.2
  177.5 3.6 collective-permute-start.4
  179.3 6.0 %collective-permute-start.5 = (f32[2,2,3,8,1,128]{5,0,3,4,1,2:T(2,128)S(1)}, f32[2,2,3,8,1,128]{5,0,3,4,1,2:T(2,128)S(1)}, u32[]{:S(2)}, u32[]{:S(2)}) collective-permute-start(f32[2,2,3,8,1,128]{5,0,3,4,1,2:T(2,128)S(1)} %get-tuple-element.88), channel_id=1, source_target_pairs={{16,0},{17,1},{18,2},{19,3},{20,4},{21,5},{22,6},{23,7},{24,8},{25... | collective-permute-start | bytes 147464 | tf_op jit(solution)/shard_map/ppermute | solution.py:21
  186.1 2.8 collective-permute-start.6
  187.4 3.9 collective-permute-start.7
  199.9 1.4 copy-start.3
  267.0 6.9 %collective-permute-start.8 = (f32[2,2,3,8,1,128]{5,0,3,4,1,2:T(2,128)S(1)}, f32[2,2,3,8,1,128]{5,0,3,4,1,2:T(2,128)S(1)}, u32[]{:S(2)}, u32[]{:S(2)}) collective-permute-start(f32[2,2,3,8,1,128]{5,0,3,4,1,2:T(2,128)S(1)} %get-tuple-element.85), channel_id=1, source_target_pairs={{0,16},{1,17},{2,18},{3,19},{4,20},{5,21},{6,22},{7,23},{8,24},{9,... | collective-permute-start | bytes 147464 | tf_op jit(solution)/shard_map/ppermute | solution.py:20
  268.9 6.0 %collective-permute-start.9 = (f32[2,2,3,8,1,128]{5,0,3,4,1,2:T(2,128)S(1)}, f32[2,2,3,8,1,128]{5,0,3,4,1,2:T(2,128)S(1)}, u32[]{:S(2)}, u32[]{:S(2)}) collective-permute-start(f32[2,2,3,8,1,128]{5,0,3,4,1,2:T(2,128)S(1)} %get-tuple-element.86), channel_id=1, source_target_pairs={{16,0},{17,1},{18,2},{19,3},{20,4},{21,5},{22,6},{23,7},{24,8},{25... | collective-permute-start | bytes 147464 | tf_op jit(solution)/shard_map/ppermute | solution.py:21
  275.7 3.1 collective-permute-start.10
  277.0 3.9 collective-permute-start.11
  289.5 1.4 copy-start.4
  341.4 5.4 %collective-permute-start.12 = (f32[2,2,3,8,1,128]{5,0,3,4,1,2:T(2,128)S(1)}, f32[2,2,3,8,1,128]{5,0,3,4,1,2:T(2,128)S(1)}, u32[]{:S(2)}, u32[]{:S(2)}) collective-permute-start(f32[2,2,3,8,1,128]{5,0,3,4,1,2:T(2,128)S(1)} %get-tuple-element.83), channel_id=1, source_target_pairs={{0,16},{1,17},{2,18},{3,19},{4,20},{5,21},{6,22},{7,23},{8,24},{9,... | collective-permute-start | bytes 147464 | tf_op jit(solution)/shard_map/ppermute | solution.py:20
  345.1 6.0 %collective-permute-start.13 = (f32[2,2,3,8,1,128]{5,0,3,4,1,2:T(2,128)S(1)}, f32[2,2,3,8,1,128]{5,0,3,4,1,2:T(2,128)S(1)}, u32[]{:S(2)}, u32[]{:S(2)}) collective-permute-start(f32[2,2,3,8,1,128]{5,0,3,4,1,2:T(2,128)S(1)} %get-tuple-element.84), channel_id=1, source_target_pairs={{16,0},{17,1},{18,2},{19,3},{20,4},{21,5},{22,6},{23,7},{24,8},{25... | collective-permute-start | bytes 147464 | tf_op jit(solution)/shard_map/ppermute | solution.py:21
  351.9 2.8 collective-permute-start.14
  353.2 3.8 collective-permute-start.15
  365.6 1.4 copy-start.5
  418.9 4.0 copy-start
Sparse Core Ops, SparseCore 0:
  9.6 39.7 all-gather.2
  96.1 36.5 all-gather.4
where the time goes:
time: 439 us; the launch traced here: 435 us
  blocking collectives  233 us (53%)
  matrix products  50.6 us (12%)
  other arithmetic  50.2 us (11%)
  waiting for transfers between devices  49 us (11%)
  starting transfers between devices  26.2 us (6%)
  between operations  15.2 us (3%)
  local copies, waits for them, and re-layouts  11.1 us (3%)
    psum x4, blocking collectives, on_device(): g_raw = lax.psum(inner_basis(all_images, work), ('gx', 'gy'))  85.8 us
    psum x4, blocking collectives, on_device(): h_next = jnp.sqrt(lax.psum(per_source(work, work), ('gx', 'gy')) + eps)  47.2 us
    psum x4, blocking collectives, on_device(): lax.psum(jnp.stack([per_source(vec, work) for vec in krylov]), ('gx', 'gy'))  47.2 us
    dot_general x8, matrix products, combine(): jnp.einsum('ks,kpczxy->spczxy', coeffs, vectors, precision=lax.Precision....  24.5 us
    all_gather x1, waiting for transfers between devices, on_device(): lax.all_gather(images, 'tx', axis=0, tiled=True)  24.5 us
    psum x2, blocking collectives, on_device(): lax.psum(per_source(residual, residual), ('gx', 'gy')) + eps  23.6 us
    ppermute x8, waiting for transfers between devices, with_halo(): after = lax.ppermute(initial, axis, down)  22.6 us
    dot_general x5, matrix products, inner_basis(): jnp.einsum('kpczxy,spczxy->ks', vectors, field, precision=lax.Precision.H...  18.3 us
  transfers between devices with their start and end apart: 18, of which 14 were waited for; matrix products, arithmetic and copies ran while one was open for 10% of the time, Pallas kernels for 0%

commit v1 on v0

v1 whole, which is shorter than its diff:
```python
import functools

import jax
import jax.numpy as jnp
from jax import lax
from jax.experimental import pallas as pl
from jax.experimental.pallas import tpu as pltpu
from jax.sharding import PartitionSpec as P

CYCLES = 2
ARNOLDI = 2
EPS = 1e-06
MESH = pl.DeviceIdType.MESH
F32 = jnp.float32


def kernel(
    dims, pos_ref, u_ref, c_ref, m_ref, sol_ref, res_ref,
    full_c, full_u, ind_all, induct, krylov, work, total, inverse, coef, outer,
    part, parts, row_out, row_in, col_out, col_in,
    gather_send, gather_recv, ind_send, ind_recv, sum_send, sum_recv, halo_send, halo_recv,
):
    n_gx, n_gy, n_tx = dims
    gx, gy, tx = lax.axis_index("gx"), lax.axis_index("gy"), lax.axis_index("tx")
    group = n_gx * n_gy
    rank = gx * n_gy + gy
    sources = pos_ref.shape[0]
    per_dev = c_ref.shape[0]
    rows = c_ref.shape[1]
    width_y = c_ref.shape[2]
    width_x = 8
    depth = induct.shape[1]
    tiles = rows // width_x
    vecs = full_c.shape[0]
    half = tiles // 2
    resid = res_ref

    def peer_of(offset):
        other = lax.rem(rank + offset, group)
        return (lax.div(other, n_gy), lax.rem(other, n_gy), tx)

    def along(offset):
        return (gx, gy, lax.rem(tx + offset, n_tx))

    barrier = pltpu.get_barrier_semaphore()
    for offset in range(1, group):
        pl.semaphore_signal(barrier, inc=1, device_id=peer_of(offset), device_id_type=MESH)
    for offset in range(1, n_tx):
        pl.semaphore_signal(barrier, inc=1, device_id=along(offset), device_id_type=MESH)
    pl.semaphore_wait(barrier, group - 1 + n_tx - 1)

    def slot(shard):
        return pl.ds(shard * per_dev, per_dev)

    def hop(which, way, step):
        full = (full_c, full_u)[which]
        sign = 1 if way == 0 else -1
        shard = tx - sign * (step - 1)
        source = (c_ref, u_ref)[which] if step == 1 else full.at[slot(shard)]
        return pltpu.make_async_remote_copy(
            src_ref=source,
            dst_ref=full.at[slot(shard)],
            send_sem=gather_send.at[which, way, step - 1],
            recv_sem=gather_recv.at[which, way, step - 1],
            device_id=(gx, gy, tx + sign),
            device_id_type=MESH,
        )

    def sends(way, step):
        if way == 0:
            return jnp.logical_and(tx + 1 < n_tx, tx - step + 1 >= 0)
        return jnp.logical_and(tx - 1 >= 0, tx + step - 1 < n_tx)

    def receives(way, step):
        return tx - step >= 0 if way == 0 else tx + step < n_tx

    def gather_start(which, step):
        for way in range(2):
            @pl.when(sends(way, step))
            def _():
                hop(which, way, step).start()

    def gather_arrive(which, step):
        for way in range(2):
            @pl.when(receives(way, step))
            def _():
                full = (full_c, full_u)[which]
                shard = tx - step if way == 0 else tx + step
                pltpu.make_async_remote_copy(
                    src_ref=(c_ref, u_ref)[which],
                    dst_ref=full.at[slot(shard)],
                    send_sem=gather_send.at[which, way, step - 1],
                    recv_sem=gather_recv.at[which, way, step - 1],
                    device_id=along(1),
                    device_id_type=MESH,
                ).wait_recv()

    def gather_sent(which):
        for step in range(1, n_tx):
            for way in range(2):
                @pl.when(sends(way, step))
                def _():
                    hop(which, way, step).wait_send()

    def ind_copy(offset):
        return pltpu.make_async_remote_copy(
            src_ref=m_ref,
            dst_ref=ind_all.at[tx],
            send_sem=ind_send.at[offset - 1],
            recv_sem=ind_recv.at[offset - 1],
            device_id=along(offset),
            device_id_type=MESH,
        )

    for offset in range(1, n_tx):
        ind_copy(offset).start()
    gather_start(0, 1)
    ind_all[pl.ds(tx, 1)] = m_ref[...][None]
    full_c[slot(tx)] = c_ref[...]
    full_u[slot(tx)] = u_ref[...]
    for offset in range(1, n_tx):
        ind_copy(offset).wait()
    layers = depth // n_tx
    for owner in range(n_tx):
        piece = ind_all[owner].astype(F32).reshape(3, layers, width_x, width_y)
        for layer in range(layers):
            induct[:, owner * layers + layer] = piece[:, layer]

    size_x, size_y = width_x * n_gx, width_y * n_gy
    shape = (depth, width_x, width_y)
    z_pos = lax.broadcasted_iota(jnp.int32, shape, 0).astype(F32)
    x_pos = (gx * width_x + lax.broadcasted_iota(jnp.int32, shape, 1)).astype(F32)
    y_pos = (gy * width_y + lax.broadcasted_iota(jnp.int32, shape, 2)).astype(F32)
    for s in range(sources):
        d_z, d_x, d_y = z_pos - pos_ref[s, 0], x_pos - pos_ref[s, 1], y_pos - pos_ref[s, 2]
        dist = jnp.sqrt(d_z * d_z + d_x * d_x + d_y * d_y)
        primary = jnp.exp(-dist / ((size_x + size_y) / 8.0))
        for comp, weight in enumerate((1.0, 0.5, 0.25)):
            real = (induct[comp] - 1.0) * weight * primary
            resid[s, pl.ds(comp * depth, depth)] = real
            resid[s, pl.ds(half + comp * depth, depth)] = 0.5 * real
    for step in range(2, n_tx):
        gather_arrive(0, step - 1)
        gather_start(0, step)
    gather_arrive(0, n_tx - 1)
    gather_start(1, 1)

    def sum_copy(index, count, offset):
        return pltpu.make_async_remote_copy(
            src_ref=part.at[index, pl.ds(0, count)],
            dst_ref=parts.at[index, rank, pl.ds(0, count)],
            send_sem=sum_send.at[index, offset - 1],
            recv_sem=sum_recv.at[index, offset - 1],
            device_id=peer_of(offset),
            device_id_type=MESH,
        )

    def group_sum(index, count):
        for offset in range(1, group):
            sum_copy(index, count, offset).start()
        parts[index, pl.ds(rank, 1), pl.ds(0, count)] = part[index, pl.ds(0, count)][None]
        for offset in range(1, group):
            sum_copy(index, count, offset).wait()
        return jnp.sum(parts[index, :, pl.ds(0, count)], axis=0)

    def images_inner(index, base, field):
        def body(k, _):
            vector = full_c[k].astype(F32).reshape(tiles, width_x, width_y)
            for s in range(sources):
                product = jnp.sum(vector * field[s], axis=0)
                part[index, pl.ds(base + s * vecs + k, 1)] = jnp.sum(product, axis=0, keepdims=True)
            return 0

        lax.fori_loop(0, vecs, body, 0)

    def inner(index, row, left, right, s):
        product = jnp.sum(left[s] * right[s], axis=0)
        part[index, pl.ds(row, 1)] = jnp.sum(product, axis=0, keepdims=True)

    def spread(value):
        return jnp.broadcast_to(value, (width_x, width_y))

    def combine(out, terms, rows_of, stack, extra=None):
        for s in range(sources):
            for k in range(vecs):
                coef[s, k] = spread(rows_of[s][:, k : k + 1])
        wide = [[spread(c[s]) for s in range(sources)] for _, c in terms]
        wide_extra = [[spread(c[s]) for s in range(sources)] for _, c in extra[1]] if extra else []

        def body(j, _):
            at = pl.ds(pl.multiple_of(j * 16, 16), 16)
            pair = pl.ds(j * 2, 2)
            totals = []
            for s in range(sources):
                value = None
                for (ref, _), w in zip(terms, wide):
                    now = ref[s, pair] * w[s][None]
                    value = now if value is None else value + now
                totals.append(value)
            if extra:
                out2, terms2, keep = extra
                for s in range(sources):
                    value = out2[s, pair] if keep else None
                    for (ref, _), w in zip(terms2, wide_extra):
                        now = ref[s, pair] * w[s][None]
                        value = now if value is None else value + now
                    out2[s, pair] = value
            for k in range(vecs):
                vector = stack[k, at, :].astype(F32).reshape(2, width_x, width_y)
                for s in range(sources):
                    totals[s] = totals[s] + vector * coef[s, k][None]
            for s in range(sources):
                out[s, pair] = totals[s]
            return 0

        lax.fori_loop(0, tiles // 2, body, 0)

    east, west = gx + 1 < n_gx, gx >= 1
    north, south = gy + 1 < n_gy, gy >= 1
    lane2 = lax.broadcasted_iota(jnp.int32, (depth, width_y), 1)
    layer2 = lax.broadcasted_iota(jnp.int32, (depth, width_y), 0)
    layer3 = lax.broadcasted_iota(jnp.int32, shape, 0)
    row3 = lax.broadcasted_iota(jnp.int32, shape, 1)
    lane3 = lax.broadcasted_iota(jnp.int32, shape, 2)
    both = jnp.logical_and
    links = (
        (row_out, 1, row_in, 0, (1, 0), east, west),
        (row_out, 0, row_in, 1, (-1, 0), west, east),
        (col_out, 1, col_in, 0, (0, 1), north, south),
        (col_out, 0, col_in, 1, (0, -1), south, north),
        (col_out, 1, col_in, 2, (-1, 1), both(west, north), both(east, south)),
        (col_out, 0, col_in, 3, (1, -1), both(east, south), both(west, north)),
    )

    def halo_copy(index, number):
        src, which, dst, place, (d_x, d_y), _, _ = links[number]
        return pltpu.make_async_remote_copy(
            src_ref=src.at[index, which],
            dst_ref=dst.at[index, place],
            send_sem=halo_send.at[index, number],
            recv_sem=halo_recv.at[index, number],
            device_id=(gx + d_x, gy + d_y, tx),
            device_id_type=MESH,
        )

    def exchange(index, field):
        lanes = lax.broadcasted_iota(jnp.int32, (tiles, width_x, width_y), 2)
        places = lax.broadcasted_iota(jnp.int32, (tiles, width_x, width_y), 0)
        first = jnp.zeros((width_x, width_y), F32)
        last = jnp.zeros((width_x, width_y), F32)
        for s in range(sources):
            value = field[s]
            here = lanes == places + s * tiles
            first = first + jnp.sum(jnp.where(here, value[:, :, 0:1], 0.0), axis=0)
            last = last + jnp.sum(jnp.where(here, value[:, :, width_y - 1 : width_y], 0.0), axis=0)
            row_out[index, 0, pl.ds(s * tiles, tiles)] = value[:, 0, :]
            row_out[index, 1, pl.ds(s * tiles, tiles)] = value[:, width_x - 1, :]
        col_out[index, 0] = first
        col_out[index, 1] = last
        for number in range(len(links)):
            @pl.when(links[number][5])
            def _():
                halo_copy(index, number).start()
        for number in range(len(links)):
            dst, place, got = links[number][2], links[number][3], links[number][6]

            @pl.when(jnp.logical_not(got))
            def _():
                dst[index, place] = jnp.zeros(dst.shape[2:], F32)

            @pl.when(got)
            def _():
                halo_copy(index, number).wait_recv()

    def apply(index, field, out):
        exchange(index, field)

        def columns(place, at):
            packed = col_in[index, place][None]
            return jnp.sum(jnp.where(lane3 == layer3 + at, packed, 0.0), axis=2, keepdims=True)

        def corner(place, row, at):
            packed = col_in[index, place, row : row + 1]
            return jnp.sum(jnp.where(lane2 == layer2 + at, packed, 0.0), axis=1, keepdims=True)

        def plus_y(f, edge):
            return jnp.where(lane3 == width_y - 1, edge, pltpu.roll(f, width_y - 1, 2))

        def minus_y(f, edge):
            return jnp.where(lane3 == 0, edge, pltpu.roll(f, 1, 2))

        def plus_x(f, row):
            return jnp.where(row3 == width_x - 1, row[:, None, :], pltpu.roll(f, width_x - 1, 1))

        def minus_x(f, row):
            return jnp.where(row3 == 0, row[:, None, :], pltpu.roll(f, 1, 1))

        zero = jnp.zeros((1, width_x, width_y), F32)

        def plus_z(f):
            return jnp.concatenate([f[1:], zero], axis=0)

        def minus_z(f):
            return jnp.concatenate([zero, f[:-1]], axis=0)

        def body(s, _):
            for p in range(2):
                def comp(c):
                    return field[s, pl.ds(p * half + c * depth, depth)]

                def at(c):
                    return s * tiles + p * half + c * depth

                def row(place, c):
                    return row_in[index, place, pl.ds(pl.multiple_of(at(c), 8), depth)]

                e_x, e_y, e_z = comp(0), comp(1), comp(2)
                xp_y = plus_y(e_x, columns(1, at(0)))
                xm_y = minus_y(e_x, columns(0, at(0)))
                t = xp_y - e_x
                hx = row(0, 0)
                hx_up = jnp.where(lane2 == width_y - 1, corner(3, width_x - 1, at(0)), pltpu.roll(hx, width_y - 1, 1))
                dt = t - minus_x(t, hx_up - hx)
                c = e_x - minus_x(e_x, hx)
                a = e_y - minus_y(e_y, columns(0, at(1)))
                hy = row(1, 1)
                hy_down = jnp.where(lane2 == 0, corner(2, 0, at(1)), pltpu.roll(hy, 1, 1))
                da = plus_x(a, hy - hy_down) - a
                y2 = plus_x(e_y, hy) + minus_x(e_y, row(0, 1)) - 2.0 * e_y
                zp_x = plus_x(e_z, row(1, 2))
                zp_y = plus_y(e_z, columns(1, at(2)))
                z2 = zp_x + minus_x(e_z, row(0, 2)) + zp_y + minus_y(e_z, columns(0, at(2))) - 4.0 * e_z
                fx_z = zp_x - e_z
                fy_z = zp_y - e_z
                k_x = da - (xp_y + xm_y + plus_z(e_x) + minus_z(e_x) - 4.0 * e_x) + (fx_z - minus_z(fx_z))
                k_y = (fy_z - minus_z(fy_z)) - (plus_z(e_y) + minus_z(e_y) - 2.0 * e_y) - y2 + dt
                ca = c + a
                k_z = (plus_z(ca) - ca) - z2
                for number, value in enumerate((k_x, k_y, k_z)):
                    cross = induct[number] * field[s, pl.ds((1 - p) * half + number * depth, depth)]
                    value = value - cross if p == 0 else value + cross
                    out[s, pl.ds(p * half + number * depth, depth)] = value
            return 0

        lax.fori_loop(0, sources, body, 0)

    total[...] = jnp.zeros_like(total)

    def gram_body(j, _):
        block = full_c[:, pl.ds(pl.multiple_of(j * 16, 16), 16), :].reshape(vecs * 16, width_y)
        total[...] += lax.dot_general(block, block, (((1,), (1,)), ((), ())), preferred_element_type=F32)
        return 0

    lax.fori_loop(0, rows // 16, gram_body, 0)
    wide = vecs * 16
    same = lax.rem(lax.broadcasted_iota(jnp.int32, (wide, wide), 0), 16) == lax.rem(
        lax.broadcasted_iota(jnp.int32, (wide, wide), 1), 16
    )
    folded = jnp.sum(jnp.where(same, total[...], 0.0).reshape(vecs, 16, wide), axis=1)
    halves = wide // width_y
    for h in range(halves):
        part[0, pl.ds(h * vecs, vecs)] = folded[:, h * width_y : (h + 1) * width_y]
    gram_rows = halves * vecs
    images_inner(0, gram_rows, resid)
    first_sum = group_sum(0, gram_rows + sources * vecs)
    gram = jnp.zeros((vecs, vecs), F32)
    for h in range(halves):
        lane = lax.broadcasted_iota(jnp.int32, (width_y, vecs), 0)
        column = lax.broadcasted_iota(jnp.int32, (width_y, vecs), 1)
        pick = (lax.div(lane, 16) + h * (width_y // 16) == column).astype(F32)
        gram = gram + jnp.dot(
            first_sum[h * vecs : (h + 1) * vecs], pick,
            precision=lax.Precision.HIGHEST, preferred_element_type=F32,
        )
    row_id = lax.broadcasted_iota(jnp.int32, (vecs, vecs), 0)
    eye = (row_id == lax.broadcasted_iota(jnp.int32, (vecs, vecs), 1)).astype(F32)
    wide_row = lax.broadcasted_iota(jnp.int32, (vecs, 2 * vecs), 0)
    system = jnp.concatenate([gram, eye], axis=1)
    for k in range(vecs):
        pivot = system[k : k + 1] / system[k : k + 1, k : k + 1]
        system = jnp.where(wide_row == k, pivot, system - system[:, k : k + 1] * pivot)
    inverse[...] = system[:, vecs:]

    def solve(column):
        answer = jnp.sum(inverse[...] * column, axis=0, keepdims=True)
        flat = jnp.sum(eye * column, axis=0, keepdims=True)
        return answer, jnp.sum(answer * flat, axis=1, keepdims=True)

    start = jnp.sum(first_sum[gram_rows:], axis=1, keepdims=True)
    weights = [solve(start[s * vecs : (s + 1) * vecs])[0] for s in range(sources)]
    one = jnp.ones((1, 1), F32)
    combine(resid, [(resid, [one] * sources)], [-w for w in weights], full_c)

    every = range(sources)
    base = sources * vecs
    for cycle in range(CYCLES):
        index = 2 * cycle
        apply(index, resid, work)
        images_inner(index + 1, 0, work)
        for s in every:
            inner(index + 1, base + 4 * s, resid, resid, s)
            inner(index + 1, base + 4 * s + 1, resid, work, s)
            inner(index + 1, base + 4 * s + 2, work, work, s)
            part[index + 1, pl.ds(base + 4 * s + 3, 1)] = jnp.zeros((1, width_y), F32)
        sums = jnp.sum(group_sum(index + 1, base + 4 * sources), axis=1, keepdims=True)
        state = []
        for s in every:
            def got(i):
                return sums[base + 4 * s + i : base + 4 * s + i + 1]

            beta = jnp.sqrt(got(0) + EPS)
            scale = 1.0 / beta
            raw, quad = solve(sums[s * vecs : (s + 1) * vecs])
            g_0 = raw * scale
            n_00 = got(0) * scale * scale
            h_00 = got(1) * scale * scale
            left = (got(2) - quad) * scale * scale - 2.0 * h_00 * h_00 + h_00 * h_00 * n_00
            left = jnp.maximum(left, 0.0)
            h_10 = jnp.sqrt(left + EPS)
            state.append((beta, scale, g_0, n_00, h_00, left, h_10))
        combine(
            krylov,
            [(work, [v[1] / v[6] for v in state]), (resid, [-v[4] * v[1] / v[6] for v in state])],
            [-v[2] / v[6] for v in state],
            full_c,
        )
        if cycle + 1 < n_tx - 1:
            gather_arrive(1, cycle + 1)
            gather_start(1, cycle + 2)
        apply(index + 1, krylov, work)
        images_inner(index + 2, 0, work)
        for s in every:
            inner(index + 2, base + 4 * s, resid, work, s)
            inner(index + 2, base + 4 * s + 1, krylov, work, s)
            inner(index + 2, base + 4 * s + 2, work, work, s)
            inner(index + 2, base + 4 * s + 3, krylov, krylov, s)
        sums = jnp.sum(group_sum(index + 2, base + 4 * sources), axis=1, keepdims=True)
        in_r, in_v, in_w, in_g, out_r, out_v = [], [], [], [], [], []
        for s in every:
            def got(i):
                return sums[base + 4 * s + i : base + 4 * s + i + 1]

            beta, scale, g_0, n_00, h_00, _, h_10 = state[s]
            g_1, quad = solve(sums[s * vecs : (s + 1) * vecs])
            h_01 = got(0) * scale
            h_11 = got(1)
            n_11 = got(3)
            n_01 = h_00 * (1.0 - n_00) / h_10
            left = (
                got(2) - quad - 2.0 * (h_01 * h_01 + h_11 * h_11)
                + h_01 * h_01 * n_00 + h_11 * h_11 * n_11 + 2.0 * h_01 * h_11 * n_01
            )
            h_21 = jnp.sqrt(jnp.maximum(left, 0.0) + EPS)
            a_00 = h_00 * h_00 + h_10 * h_10
            a_01 = h_00 * h_01 + h_10 * h_11
            a_11 = h_01 * h_01 + h_11 * h_11 + h_21 * h_21
            l_00 = jnp.sqrt(a_00)
            l_10 = a_01 / l_00
            l_11 = jnp.sqrt(a_11 - l_10 * l_10)
            f_0 = beta * h_00 / l_00
            f_1 = (beta * h_01 - l_10 * f_0) / l_11
            y_1 = f_1 / l_11
            y_0 = (f_0 - l_10 * y_1) / l_00
            t_0 = beta - h_00 * y_0 - h_01 * y_1
            t_1 = -(h_10 * y_0 + h_11 * y_1)
            t_2 = -h_21 * y_1
            share = t_2 / h_21
            in_r.append((t_0 - share * h_01) * scale)
            in_v.append(t_1 - share * h_11)
            in_w.append(share)
            in_g.append(-share * g_1)
            out_r.append(y_0 * scale)
            out_v.append(y_1)
            weights[s] = weights[s] - (g_0 * y_0 + g_1 * y_1)
        update = (sol_ref, [(resid, out_r), (krylov, out_v)], cycle > 0)
        combine(resid, [(resid, in_r), (krylov, in_v), (work, in_w)], in_g, full_c, update)

    for step in range(CYCLES + 1, n_tx - 1):
        gather_arrive(1, step)
        gather_start(1, step + 1)
    gather_arrive(1, n_tx - 1)
    combine(sol_ref, [(sol_ref, [one] * sources)], weights, full_u)
    gather_sent(0)
    gather_sent(1)
    for index in range(2 * CYCLES):
        for number in range(len(links)):
            @pl.when(links[number][5])
            def _():
                halo_copy(index, number).wait_send()


def on_device(dims, src_cell, basis, images, induction):
    n_gx, n_gy, n_tx = dims
    per_dev, _, _, depth, width_x, width_y = basis.shape
    sources = src_cell.shape[0]
    size_x, size_y = width_x * n_gx, width_y * n_gy
    rest = src_cell % (size_x * size_y)
    place = jnp.stack([src_cell // (size_x * size_y), rest // size_y, rest % size_y], axis=1)
    tiles = 6 * depth
    rows = tiles * width_x
    vecs = per_dev * n_tx
    group = n_gx * n_gy
    field = (sources, tiles, width_x, width_y)
    ind_rows = 3 * induction.shape[1] * width_x
    most = vecs * 16 // width_y * vecs + sources * vecs
    sums, halos = 2 * CYCLES + 1, 2 * CYCLES
    dma = pltpu.SemaphoreType.DMA
    vmem = pl.BlockSpec(memory_space=pltpu.VMEM)
    out = pl.pallas_call(
        functools.partial(kernel, dims),
        out_shape=(jax.ShapeDtypeStruct(field, F32),) * 2,
        in_specs=[pl.BlockSpec(memory_space=pltpu.SMEM), vmem, vmem, vmem],
        out_specs=(vmem, vmem),
        scratch_shapes=[
            pltpu.VMEM((vecs, rows, width_y), jnp.bfloat16),
            pltpu.VMEM((vecs, rows, width_y), jnp.bfloat16),
            pltpu.VMEM((n_tx, ind_rows, width_y), jnp.bfloat16),
            pltpu.VMEM((3, depth, width_x, width_y), F32),
            pltpu.VMEM(field, F32),
            pltpu.VMEM(field, F32),
            pltpu.VMEM((vecs * 16, vecs * 16), F32),
            pltpu.VMEM((vecs, vecs), F32),
            pltpu.VMEM((sources, vecs, width_x, width_y), F32),
            pltpu.VMEM((8, width_y), F32),
            pltpu.VMEM((sums, most, width_y), F32),
            pltpu.VMEM((sums, group, most, width_y), F32),
            pltpu.VMEM((halos, 2, sources * tiles, width_y), F32),
            pltpu.VMEM((halos, 2, sources * tiles, width_y), F32),
            pltpu.VMEM((halos, 2, width_x, width_y), F32),
            pltpu.VMEM((halos, 4, width_x, width_y), F32),
            dma((2, 2, n_tx - 1)),
            dma((2, 2, n_tx - 1)),
            dma((n_tx - 1,)),
            dma((n_tx - 1,)),
            dma((sums, group - 1)),
            dma((sums, group - 1)),
            dma((halos, 6)),
            dma((halos, 6)),
        ],
        compiler_params=pltpu.CompilerParams(
            collective_id=0, has_side_effects=True, vmem_limit_bytes=48 * 1024 * 1024
        ),
        cost_estimate=pl.CostEstimate(flops=400_000_000, bytes_accessed=2_000_000, transcendentals=20_000),
    )(
        place.astype(F32),
        basis.reshape(per_dev, rows, width_y),
        images.reshape(per_dev, rows, width_y),
        induction.reshape(ind_rows, width_y),
    )
    shape = (sources, 2, 3, depth, width_x, width_y)
    return tuple(o.reshape(shape) for o in out)


def solution(mesh):
    dims = (mesh.shape["gx"], mesh.shape["gy"], mesh.shape["tx"])
    spec = P("tx", None, None, None, "gx", "gy")
    return jax.shard_map(
        functools.partial(on_device, dims),
        mesh=mesh,
        in_specs=(P("tx"), spec, spec, P(None, "tx", "gx", "gy")),
        out_specs=(spec, spec),
        check_vma=False,
    )
```

time: 439 us -> 102 us (0.23)
  blocking collectives: 233 us -> 0 us
  Pallas kernels: 0 us -> 96.7 us
  matrix products: 50.6 us -> 0 us
  other arithmetic: 50.2 us -> 0.1 us
  waiting for transfers between devices: 49 us -> 0 us
  starting transfers between devices: 26.2 us -> 0 us
  between operations: 15.2 us -> 0.66 us
  local copies, waits for them, and re-layouts: 11.1 us -> 4.42 us
    psum x15 -> x0, blocking collectives: 218 us -> none  [the longest x4 85.8 us: on_device(): g_raw = lax.psum(inner_basis(all_images, work), ('gx', 'gy'))]
    pallas_call x0 -> x1, Pallas kernels: none -> 96.7 us  [on_device(): pl.pallas_call(functools.partial(kernel, dims), out_shape=(jax.ShapeDtype...]
    dot_general x18 -> x0, matrix products: 48.7 us -> none  [the longest x8 24.5 us: combine(): jnp.einsum('ks,kpczxy->spczxy', coeffs, vectors, precision=lax.Precision....]
    ppermute x16 -> x0, starting transfers between devices: 26.1 us -> none  [the longest x8 15.1 us: with_halo(): before = lax.ppermute(last, axis, up)]
    all_gather x2 -> x0, waiting for transfers between devices: 24.5 us -> none  [the longest x1 24.5 us: on_device(): lax.all_gather(images, 'tx', axis=0, tiled=True)]
    ppermute x16 -> x0, waiting for transfers between devices: 23.8 us -> none  [the longest x8 22.6 us: with_halo(): after = lax.ppermute(initial, axis, down)]
    sub x54 -> x0, other arithmetic: 19.6 us -> none  [the longest x48 17.6 us: differ(): lax.slice_in_dim(field, 1, count, axis=axis)]
    all_gather x1 -> x0, blocking collectives: 15 us -> none  [on_device(): lax.all_gather(induction, 'tx', axis=1, tiled=True)]
  transfers between devices with their start and end apart: 18 -> 0, of which waited for: 14 -> 0; matrix products, arithmetic and copies ran while one was open for 10% -> 0% of each run, Pallas kernels for 0% -> 0%
where the time goes in v1:
time: 102 us
  Pallas kernels  96.7 us (95%)
  local copies, waits for them, and re-layouts  4.42 us (4%)
    pallas_call x1, Pallas kernels, on_device(): pl.pallas_call(functools.partial(kernel, dims), out_shape=(jax.ShapeDtype...  96.7 us
    unnamed x10, local copies, waits for them, and re-layouts  4.13 us

profile of v1, /device:TPU:0, one launch (start us, length us, event | category | flops | bytes accessed | tf_op | source)
XLA Modules:
  0.0 101.9 jit_solution(77082507229019011)
XLA Ops:
  0.6 0.0 copy-start.3
  0.6 0.0 copy-start.2
  0.6 0.6 copy-done.3
  1.3 0.1 copy.6
  1.4 0.1 copy.7
  1.5 0.1 copy.8
  1.6 0.1 add_convert_fusion.pos_ref
  1.7 0.0 copy-done.2
  1.7 0.0 copy-start
  1.7 1.0 copy-done
  2.7 0.0 copy-start.1
  2.7 1.0 copy-done.1
  3.7 96.7 %shard_map.59 = (f32[2,48,8,128]{3,2,1,0:T(8,128)S(1)}, f32[2,48,8,128]{3,2,1,0:T(8,128)S(1)}) custom-call(f32[2,3]{1,0:T(2,128)S(1)} %add_convert_fusion.pos_ref, bf16[4,384,128]{2,1,0:T(8,128)(2,1)S(1)} %bitcast.13, bf16[4,384,128]{2,1,0:T(8,128)(2,1)S(1)} %bitcast.14, bf16[48,128]{1,0:T(8,128)(2,1)S(1)} %bitcast.15), custom_call_target="tpu_custom_call" | custom-call | flops 400000000 | bytes 2000000 | tf_op jit(solution)/shard_map/pallas_call | solution.py:509
  100.4 0.7 copy.11
  101.1 0.7 copy.12
  (3 shorter events, 0.0 us)
Async XLA Ops:
  0.6 0.7 copy-start.3
  0.6 1.0 %copy-start.2 = (bf16[3,2,8,128]{3,2,1,0:T(8,128)(2,1)S(1)}, bf16[3,2,8,128]{3,2,1,0:T(8,128)(2,1)}, u32[]{:S(2)}) copy-start(bf16[3,2,8,128]{3,2,1,0:T(8,128)(2,1)} %param.7) | copy-start | bytes 36868
  1.7 1.0 copy-start
  2.7 1.0 copy-start.1

commit v2 on v1

--- a/solution.py
+++ b/solution.py
@@ -18,7 +18,9 @@
     dims, pos_ref, u_ref, c_ref, m_ref, sol_ref, res_ref,
     full_c, full_u, ind_all, induct, krylov, work, total, inverse, coef, outer,
     part, parts, row_out, row_in, col_out, col_in,
-    gather_send, gather_recv, ind_send, ind_recv, sum_send, sum_recv, halo_send, halo_recv,
+    img_row_out, img_row_in, img_col_out, img_col_in, row_r, row_v, col_r, col_v,
+    own_sem, gather_send, gather_recv, ind_send, ind_recv, sum_send, sum_recv, halo_send, halo_recv,
+    img_send, img_recv,
 ):
     n_gx, n_gy, n_tx = dims
     gx, gy, tx = lax.axis_index("gx"), lax.axis_index("gy"), lax.axis_index("tx")
@@ -34,6 +36,8 @@
     vecs = full_c.shape[0]
     half = tiles // 2
     resid = res_ref
+    chunk = 16 * width_x
+    chunks = rows // chunk
 
     def peer_of(offset):
         other = lax.rem(rank + offset, group)
@@ -52,16 +56,22 @@
     def slot(shard):
         return pl.ds(shard * per_dev, per_dev)
 
-    def hop(which, way, step):
+    def rows_at(which, piece):
+        return pl.ds(piece * chunk, chunk) if which == 0 else pl.ds(0, rows)
+
+    pieces = (chunks, 1)
+
+    def hop(which, way, step, piece):
         full = (full_c, full_u)[which]
+        at = rows_at(which, piece)
         sign = 1 if way == 0 else -1
         shard = tx - sign * (step - 1)
-        source = (c_ref, u_ref)[which] if step == 1 else full.at[slot(shard)]
+        source = (c_ref, u_ref)[which].at[:, at] if step == 1 else full.at[slot(shard), at]
         return pltpu.make_async_remote_copy(
             src_ref=source,
-            dst_ref=full.at[slot(shard)],
-            send_sem=gather_send.at[which, way, step - 1],
-            recv_sem=gather_recv.at[which, way, step - 1],
+            dst_ref=full.at[slot(shard), at],
+            send_sem=gather_send.at[which, way, step - 1, piece],
+            recv_sem=gather_recv.at[which, way, step - 1, piece],
             device_id=(gx, gy, tx + sign),
             device_id_type=MESH,
         )
@@ -74,33 +84,45 @@
     def receives(way, step):
         return tx - step >= 0 if way == 0 else tx + step < n_tx
 
-    def gather_start(which, step):
+    def gather_start(which, step, piece):
         for way in range(2):
             @pl.when(sends(way, step))
             def _():
-                hop(which, way, step).start()
-
-    def gather_arrive(which, step):
+                hop(which, way, step, piece).start()
+
+    def gather_arrive(which, step, piece, then=False):
         for way in range(2):
             @pl.when(receives(way, step))
             def _():
                 full = (full_c, full_u)[which]
+                at = rows_at(which, piece)
                 shard = tx - step if way == 0 else tx + step
                 pltpu.make_async_remote_copy(
-                    src_ref=(c_ref, u_ref)[which],
-                    dst_ref=full.at[slot(shard)],
-                    send_sem=gather_send.at[which, way, step - 1],
-                    recv_sem=gather_recv.at[which, way, step - 1],
+                    src_ref=full.at[slot(shard), at],
+                    dst_ref=full.at[slot(shard), at],
+                    send_sem=gather_send.at[which, way, step - 1, piece],
+                    recv_sem=gather_recv.at[which, way, step - 1, piece],
                     device_id=along(1),
                     device_id_type=MESH,
                 ).wait_recv()
 
+            if then:
+                @pl.when(sends(way, step + 1))
+                def _():
+                    hop(which, way, step + 1, piece).start()
+
     def gather_sent(which):
-        for step in range(1, n_tx):
-            for way in range(2):
-                @pl.when(sends(way, step))
-                def _():
-                    hop(which, way, step).wait_send()
+        for piece in range(pieces[which]):
+            for step in range(1, n_tx):
+                for way in range(2):
+                    @pl.when(sends(way, step))
+                    def _():
+                        hop(which, way, step, piece).wait_send()
+
+    own = [
+        pltpu.make_async_copy(ref, full.at[slot(tx)], own_sem.at[number])
+        for number, (ref, full) in enumerate(((c_ref, full_c), (u_ref, full_u)))
+    ]
 
     def ind_copy(offset):
         return pltpu.make_async_remote_copy(
@@ -114,10 +136,11 @@
 
     for offset in range(1, n_tx):
         ind_copy(offset).start()
-    gather_start(0, 1)
+    gather_start(0, 1, 0)
+    gather_start(0, 1, 1)
+    for copy in own:
+        copy.start()
     ind_all[pl.ds(tx, 1)] = m_ref[...][None]
-    full_c[slot(tx)] = c_ref[...]
-    full_u[slot(tx)] = u_ref[...]
     for offset in range(1, n_tx):
         ind_copy(offset).wait()
     layers = depth // n_tx
@@ -132,18 +155,17 @@
     x_pos = (gx * width_x + lax.broadcasted_iota(jnp.int32, shape, 1)).astype(F32)
     y_pos = (gy * width_y + lax.broadcasted_iota(jnp.int32, shape, 2)).astype(F32)
     for s in range(sources):
-        d_z, d_x, d_y = z_pos - pos_ref[s, 0], x_pos - pos_ref[s, 1], y_pos - pos_ref[s, 2]
+        cell = pos_ref[s]
+        rest = lax.rem(cell, size_x * size_y)
+        d_z = z_pos - lax.div(cell, size_x * size_y).astype(F32)
+        d_x = x_pos - lax.div(rest, size_y).astype(F32)
+        d_y = y_pos - lax.rem(rest, size_y).astype(F32)
         dist = jnp.sqrt(d_z * d_z + d_x * d_x + d_y * d_y)
         primary = jnp.exp(-dist / ((size_x + size_y) / 8.0))
         for comp, weight in enumerate((1.0, 0.5, 0.25)):
             real = (induct[comp] - 1.0) * weight * primary
             resid[s, pl.ds(comp * depth, depth)] = real
             resid[s, pl.ds(half + comp * depth, depth)] = 0.5 * real
-    for step in range(2, n_tx):
-        gather_arrive(0, step - 1)
-        gather_start(0, step)
-    gather_arrive(0, n_tx - 1)
-    gather_start(1, 1)
 
     def sum_copy(index, count, offset):
         return pltpu.make_async_remote_copy(
@@ -155,20 +177,30 @@
             device_id_type=MESH,
         )
 
-    def group_sum(index, count):
+    def group_send(index, count):
         for offset in range(1, group):
             sum_copy(index, count, offset).start()
         parts[index, pl.ds(rank, 1), pl.ds(0, count)] = part[index, pl.ds(0, count)][None]
+
+    def group_sum(index, count):
         for offset in range(1, group):
             sum_copy(index, count, offset).wait()
         return jnp.sum(parts[index, :, pl.ds(0, count)], axis=0)
 
-    def images_inner(index, base, field):
+    def images_inner(index, base, field, piece=None):
+        size = tiles if piece is None else 16
+        at = 0 if piece is None else piece * 16
+
         def body(k, _):
-            vector = full_c[k].astype(F32).reshape(tiles, width_x, width_y)
+            vector = full_c[k, pl.ds(at * width_x, size * width_x)]
+            vector = vector.astype(F32).reshape(size, width_x, width_y)
             for s in range(sources):
-                product = jnp.sum(vector * field[s], axis=0)
-                part[index, pl.ds(base + s * vecs + k, 1)] = jnp.sum(product, axis=0, keepdims=True)
+                product = jnp.sum(vector * field[s, pl.ds(at, size)], axis=0)
+                product = jnp.sum(product, axis=0, keepdims=True)
+                place = pl.ds(base + s * vecs + k, 1)
+                if piece:
+                    product = product + part[index, place]
+                part[index, place] = product
             return 0
 
         lax.fori_loop(0, vecs, body, 0)
@@ -243,9 +275,10 @@
             device_id_type=MESH,
         )
 
-    def exchange(index, field):
-        lanes = lax.broadcasted_iota(jnp.int32, (tiles, width_x, width_y), 2)
-        places = lax.broadcasted_iota(jnp.int32, (tiles, width_x, width_y), 0)
+    lanes = lax.broadcasted_iota(jnp.int32, (tiles, width_x, width_y), 2)
+    places = lax.broadcasted_iota(jnp.int32, (tiles, width_x, width_y), 0)
+
+    def exchange_start(index, field):
         first = jnp.zeros((width_x, width_y), F32)
         last = jnp.zeros((width_x, width_y), F32)
         for s in range(sources):
@@ -261,6 +294,8 @@
             @pl.when(links[number][5])
             def _():
                 halo_copy(index, number).start()
+
+    def exchange_wait(index):
         for number in range(len(links)):
             dst, place, got = links[number][2], links[number][3], links[number][6]
 
@@ -272,15 +307,116 @@
             def _():
                 halo_copy(index, number).wait_recv()
 
-    def apply(index, field, out):
-        exchange(index, field)
-
+    def image_copy(number, piece):
+        _, which, _, place, (d_x, d_y), _, _ = links[number]
+        if number < 2:
+            src, dst, sem = img_row_out.at[which, piece], img_row_in.at[place, piece], number * chunks + piece
+        else:
+            src, dst, sem = img_col_out.at[which], img_col_in.at[place], 2 * chunks + number - 2
+        return pltpu.make_async_remote_copy(
+            src_ref=src,
+            dst_ref=dst,
+            send_sem=img_send.at[sem],
+            recv_sem=img_recv.at[sem],
+            device_id=(gx + d_x, gy + d_y, tx),
+            device_id_type=MESH,
+        )
+
+    image_copies = [(number, piece) for number in range(2) for piece in range(chunks)]
+    image_copies += [(number, 0) for number in range(2, len(links))]
+
+    def image_start(number, piece):
+        @pl.when(links[number][5])
+        def _():
+            image_copy(number, piece).start()
+
+    def image_pack(piece):
+        size = (16, width_x, width_y)
+        lane = lax.broadcasted_iota(jnp.int32, size, 2)
+        tile = lax.broadcasted_iota(jnp.int32, size, 0) + piece * 16
+        here = lane == tile
+        for s in range(1, sources):
+            here = jnp.logical_or(here, lane == tile + s * tiles)
+
+        def body(k, _):
+            value = full_c[k, pl.ds(piece * chunk, chunk)].astype(F32).reshape(size)
+            for side, (row, col) in enumerate(((0, 0), (width_x - 1, width_y - 1))):
+                img_row_out[side, piece, pl.ds(pl.multiple_of(k * 16, 16), 16)] = value[:, row, :]
+                column = jnp.sum(jnp.where(here, value[:, :, col : col + 1], 0.0), axis=0)
+                if piece:
+                    column = column + img_col_out[side, k]
+                img_col_out[side, k] = column
+            return 0
+
+        lax.fori_loop(0, vecs, body, 0)
+        for number in range(2):
+            image_start(number, piece)
+
+    def image_wait():
+        for number, piece in image_copies:
+            place, got = links[number][3], links[number][6]
+
+            @pl.when(jnp.logical_not(got))
+            def _():
+                if number < 2:
+                    img_row_in[place, piece] = jnp.zeros(img_row_in.shape[2:], F32)
+                else:
+                    img_col_in[place] = jnp.zeros(img_col_in.shape[1:], F32)
+
+            @pl.when(got)
+            def _():
+                image_copy(number, piece).wait_recv()
+
+    def by_lane(values):
+        lane = lax.broadcasted_iota(jnp.int32, (width_x, width_y), 1)
+        result = values[0]
+        for s in range(1, sources):
+            result = jnp.where(lane >= s * tiles, values[s], result)
+        return result
+
+    def combine_halo(row, col, terms):
+        wide = [[spread(c[s]) for s in range(sources)] for _, _, c in terms]
+
+        def body(i, _):
+            place, piece = lax.div(i, chunks), lax.rem(i, chunks)
+            totals = []
+            for s in range(sources):
+                at = pl.ds(pl.multiple_of(s * tiles + piece * 16, 8), 16)
+                value = None
+                for (ref, _, _), w in zip(terms, wide):
+                    now = ref[place, at].reshape(2, width_x, width_y) * w[s][None]
+                    value = now if value is None else value + now
+                totals.append(value)
+            for k in range(vecs):
+                vector = img_row_in[place, piece, pl.ds(k * 16, 16)].reshape(2, width_x, width_y)
+                for s in range(sources):
+                    totals[s] = totals[s] + vector * coef[s, k][None]
+            for s in range(sources):
+                at = pl.ds(pl.multiple_of(s * tiles + piece * 16, 8), 16)
+                row[place, at] = totals[s].reshape(16, width_y)
+            return 0
+
+        lax.fori_loop(0, 2 * chunks, body, 0)
+        values = [None] * 4
+        for (_, ref, _), w in zip(terms, wide):
+            scale = by_lane(w)
+            for place in range(4):
+                now = ref[place] * scale
+                values[place] = now if values[place] is None else values[place] + now
+        for k in range(vecs):
+            scale = by_lane([coef[s, k] for s in range(sources)])
+            for place in range(4):
+                values[place] = values[place] + img_col_in[place, k] * scale
+        for place in range(4):
+            col[place] = values[place]
+
+    def apply(field, row_halo, col_halo, out):
         def columns(place, at):
-            packed = col_in[index, place][None]
+            packed = col_halo[place][None]
             return jnp.sum(jnp.where(lane3 == layer3 + at, packed, 0.0), axis=2, keepdims=True)
 
         def corner(place, row, at):
-            packed = col_in[index, place, row : row + 1]
+            packed = col_halo[place, row : row + 1]
             return jnp.sum(jnp.where(lane2 == layer2 + at, packed, 0.0), axis=1, keepdims=True)
 
         def plus_y(f, edge):
@@ -312,7 +448,7 @@
                     return s * tiles + p * half + c * depth
 
                 def row(place, c):
-                    return row_in[index, place, pl.ds(pl.multiple_of(at(c), 8), depth)]
+                    return row_halo[place, pl.ds(pl.multiple_of(at(c), 8), depth)]
 
                 e_x, e_y, e_z = comp(0), comp(1), comp(2)
                 xp_y = plus_y(e_x, columns(1, at(0)))
@@ -344,6 +480,7 @@
 
         lax.fori_loop(0, sources, body, 0)
 
+    exchange_start(0, resid)
     total[...] = jnp.zeros_like(total)
 
     def gram_body(j, _):
@@ -351,17 +488,32 @@
         total[...] += lax.dot_general(block, block, (((1,), (1,)), ((), ())), preferred_element_type=F32)
         return 0
 
-    lax.fori_loop(0, rows // 16, gram_body, 0)
     wide = vecs * 16
+    halves = wide // width_y
+    gram_rows = halves * vecs
+    own[0].wait()
+    for piece in range(chunks):
+        for step in range(1, n_tx - 1):
+            gather_arrive(0, step, piece, True)
+        if piece + 2 < chunks:
+            gather_start(0, 1, piece + 2)
+        elif piece + 1 == chunks:
+            gather_start(1, 1, 0)
+        gather_arrive(0, n_tx - 1, piece)
+        lax.fori_loop(piece * (chunk // 16), (piece + 1) * (chunk // 16), gram_body, 0)
+        images_inner(0, gram_rows, resid, piece)
+        if piece + 1 < chunks:
+            image_pack(piece)
     same = lax.rem(lax.broadcasted_iota(jnp.int32, (wide, wide), 0), 16) == lax.rem(
         lax.broadcasted_iota(jnp.int32, (wide, wide), 1), 16
     )
     folded = jnp.sum(jnp.where(same, total[...], 0.0).reshape(vecs, 16, wide), axis=1)
-    halves = wide // width_y
     for h in range(halves):
         part[0, pl.ds(h * vecs, vecs)] = folded[:, h * width_y : (h + 1) * width_y]
-    gram_rows = halves * vecs
-    images_inner(0, gram_rows, resid)
+    group_send(0, gram_rows + sources * vecs)
+    image_pack(chunks - 1)
+    for number in range(2, len(links)):
+        image_start(number, 0)
     first_sum = group_sum(0, gram_rows + sources * vecs)
     gram = jnp.zeros((vecs, vecs), F32)
     for h in range(halves):
@@ -390,18 +542,23 @@
     weights = [solve(start[s * vecs : (s + 1) * vecs])[0] for s in range(sources)]
     one = jnp.ones((1, 1), F32)
     combine(resid, [(resid, [one] * sources)], [-w for w in weights], full_c)
+    exchange_wait(0)
+    image_wait()
+    combine_halo(row_r, col_r, [(row_in.at[0], col_in.at[0], [one] * sources)])
 
     every = range(sources)
     base = sources * vecs
     for cycle in range(CYCLES):
         index = 2 * cycle
-        apply(index, resid, work)
+        apply(resid, row_r, col_r, work)
+        exchange_start(index + 1, work)
         images_inner(index + 1, 0, work)
         for s in every:
             inner(index + 1, base + 4 * s, resid, resid, s)
             inner(index + 1, base + 4 * s + 1, resid, work, s)
             inner(index + 1, base + 4 * s + 2, work, work, s)
             part[index + 1, pl.ds(base + 4 * s + 3, 1)] = jnp.zeros((1, width_y), F32)
+        group_send(index + 1, base + 4 * sources)
         sums = jnp.sum(group_sum(index + 1, base + 4 * sources), axis=1, keepdims=True)
         state = []
         for s in every:
@@ -418,22 +575,24 @@
             left = jnp.maximum(left, 0.0)
             h_10 = jnp.sqrt(left + EPS)
             state.append((beta, scale, g_0, n_00, h_00, left, h_10))
-        combine(
-            krylov,
-            [(work, [v[1] / v[6] for v in state]), (resid, [-v[4] * v[1] / v[6] for v in state])],
-            [-v[2] / v[6] for v in state],
-            full_c,
-        )
+        of_w = [v[1] / v[6] for v in state]
+        of_r = [-v[4] * v[1] / v[6] for v in state]
+        combine(krylov, [(work, of_w), (resid, of_r)], [-v[2] / v[6] for v in state], full_c)
+        exchange_wait(index + 1)
+        now = (row_in.at[index + 1], col_in.at[index + 1])
+        combine_halo(row_v, col_v, [now + (of_w,), (row_r, col_r, of_r)])
         if cycle + 1 < n_tx - 1:
-            gather_arrive(1, cycle + 1)
-            gather_start(1, cycle + 2)
-        apply(index + 1, krylov, work)
+            gather_arrive(1, cycle + 1, 0, True)
+        apply(krylov, row_v, col_v, work)
+        if cycle + 1 < CYCLES:
+            exchange_start(index + 2, work)
         images_inner(index + 2, 0, work)
         for s in every:
             inner(index + 2, base + 4 * s, resid, work, s)
             inner(index + 2, base + 4 * s + 1, krylov, work, s)
             inner(index + 2, base + 4 * s + 2, work, work, s)
             inner(index + 2, base + 4 * s + 3, krylov, krylov, s)
+        group_send(index + 2, base + 4 * sources)
         sums = jnp.sum(group_sum(index + 2, base + 4 * sources), axis=1, keepdims=True)
         in_r, in_v, in_w, in_g, out_r, out_v = [], [], [], [], [], []
         for s in every:
@@ -474,11 +633,15 @@
             weights[s] = weights[s] - (g_0 * y_0 + g_1 * y_1)
         update = (sol_ref, [(resid, out_r), (krylov, out_v)], cycle > 0)
         combine(resid, [(resid, in_r), (krylov, in_v), (work, in_w)], in_g, full_c, update)
+        if cycle + 1 < CYCLES:
+            exchange_wait(index + 2)
+            now = (row_in.at[index + 2], col_in.at[index + 2])
+            combine_halo(row_r, col_r, [(row_r, col_r, in_r), (row_v, col_v, in_v), now + (in_w,)])
 
     for step in range(CYCLES + 1, n_tx - 1):
-        gather_arrive(1, step)
-        gather_start(1, step + 1)
-    gather_arrive(1, n_tx - 1)
+        gather_arrive(1, step, 0, True)
+    gather_arrive(1, n_tx - 1, 0)
+    own[1].wait()
     combine(sol_ref, [(sol_ref, [one] * sources)], weights, full_u)
     gather_sent(0)
     gather_sent(1)
@@ -487,15 +650,16 @@
             @pl.when(links[number][5])
             def _():
                 halo_copy(index, number).wait_send()
+    for number, piece in image_copies:
+        @pl.when(links[number][5])
+        def _():
+            image_copy(number, piece).wait_send()
 
 
 def on_device(dims, src_cell, basis, images, induction):
     n_gx, n_gy, n_tx = dims
     per_dev, _, _, depth, width_x, width_y = basis.shape
     sources = src_cell.shape[0]
-    size_x, size_y = width_x * n_gx, width_y * n_gy
-    rest = src_cell % (size_x * size_y)
-    place = jnp.stack([src_cell // (size_x * size_y), rest // size_y, rest % size_y], axis=1)
     tiles = 6 * depth
     rows = tiles * width_x
     vecs = per_dev * n_tx
@@ -506,10 +670,12 @@
     sums, halos = 2 * CYCLES + 1, 2 * CYCLES
     dma = pltpu.SemaphoreType.DMA
     vmem = pl.BlockSpec(memory_space=pltpu.VMEM)
+    hbm = pl.BlockSpec(memory_space=pl.ANY)
+    chunks = tiles // 16
     out = pl.pallas_call(
         functools.partial(kernel, dims),
         out_shape=(jax.ShapeDtypeStruct(field, F32),) * 2,
-        in_specs=[pl.BlockSpec(memory_space=pltpu.SMEM), vmem, vmem, vmem],
+        in_specs=[pl.BlockSpec(memory_space=pltpu.SMEM), hbm, hbm, vmem],
         out_specs=(vmem, vmem),
         scratch_shapes=[
             pltpu.VMEM((vecs, rows, width_y), jnp.bfloat16),
@@ -528,21 +694,32 @@
             pltpu.VMEM((halos, 2, sources * tiles, width_y), F32),
             pltpu.VMEM((halos, 2, width_x, width_y), F32),
             pltpu.VMEM((halos, 4, width_x, width_y), F32),
-            dma((2, 2, n_tx - 1)),
-            dma((2, 2, n_tx - 1)),
+            pltpu.VMEM((2, chunks, vecs * 16, width_y), F32),
+            pltpu.VMEM((2, chunks, vecs * 16, width_y), F32),
+            pltpu.VMEM((2, vecs, width_x, width_y), F32),
+            pltpu.VMEM((4, vecs, width_x, width_y), F32),
+            pltpu.VMEM((2, sources * tiles, width_y), F32),
+            pltpu.VMEM((2, sources * tiles, width_y), F32),
+            pltpu.VMEM((4, width_x, width_y), F32),
+            pltpu.VMEM((4, width_x, width_y), F32),
+            dma((2,)),
+            dma((2, 2, n_tx - 1, chunks)),
+            dma((2, 2, n_tx - 1, chunks)),
             dma((n_tx - 1,)),
             dma((n_tx - 1,)),
             dma((sums, group - 1)),
             dma((sums, group - 1)),
             dma((halos, 6)),
             dma((halos, 6)),
+            dma((2 * chunks + 4,)),
+            dma((2 * chunks + 4,)),
         ],
         compiler_params=pltpu.CompilerParams(
             collective_id=0, has_side_effects=True, vmem_limit_bytes=48 * 1024 * 1024
         ),
         cost_estimate=pl.CostEstimate(flops=400_000_000, bytes_accessed=2_000_000, transcendentals=20_000),
     )(
-        place.astype(F32),
+        src_cell,
         basis.reshape(per_dev, rows, width_y),
         images.reshape(per_dev, rows, width_y),
         induction.reshape(ind_rows, width_y),

time: 102 us -> 88.5 us (0.87)
  Pallas kernels: 96.7 us -> 82.8 us
    pallas_call x1, Pallas kernels: 96.7 us -> 82.8 us  [on_device(): pl.pallas_call(functools.partial(kernel, dims), out_shape=(jax.ShapeDtype...]
where the time goes in v2:
time: 88.5 us; the launch traced here: 88.2 us
  Pallas kernels  82.8 us (94%)
  local copies, waits for them, and re-layouts  4.84 us (5%)
    pallas_call x1, Pallas kernels, on_device(): pl.pallas_call(functools.partial(kernel, dims), out_shape=(jax.ShapeDtype...  82.8 us
    unnamed x10, local copies, waits for them, and re-layouts  4.84 us

profile of v2, /device:TPU:0, one launch (start us, length us, event | category | flops | bytes accessed | tf_op | source)
XLA Modules:
  0.0 88.2 jit_solution(6954820574093757957)
XLA Ops:
  0.6 0.0 copy-start.3
  0.6 0.6 copy-done.3
  1.3 0.0 copy-start
  1.3 1.0 %copy-done = bf16[4,2,3,8,8,128]{5,4,3,2,1,0:T(8,128)(2,1)S(1)} copy-done((bf16[4,2,3,8,8,128]{5,4,3,2,1,0:T(8,128)(2,1)S(1)}, bf16[4,2,3,8,8,128]{5,4,3,2,1,0:T(8,128)(2,1)}, u32[]{:S(2)}) %copy-start) | copy-done | bytes 393240
  2.3 0.0 copy-start.1
  2.3 1.0 %copy-done.1 = bf16[4,2,3,8,8,128]{5,4,3,2,1,0:T(8,128)(2,1)S(1)} copy-done((bf16[4,2,3,8,8,128]{5,4,3,2,1,0:T(8,128)(2,1)S(1)}, bf16[4,2,3,8,8,128]{5,4,3,2,1,0:T(8,128)(2,1)}, u32[]{:S(2)}) %copy-start.1) | copy-done | bytes 393240
  3.3 0.0 copy-start.2
  3.3 0.7 copy-done.2
  4.0 82.8 %shard_map.59 = (f32[2,48,8,128]{3,2,1,0:T(8,128)S(1)}, f32[2,48,8,128]{3,2,1,0:T(8,128)S(1)}) custom-call(s32[2]{0:T(128)S(1)} %copy-done.3, bf16[4,384,128]{2,1,0:T(8,128)(2,1)S(1)} %bitcast.7, bf16[4,384,128]{2,1,0:T(8,128)(2,1)S(1)} %bitcast.8, bf16[48,128]{1,0:T(8,128)(2,1)S(1)} %bitcast.9), custom_call_target="tpu_custom_call" | custom-call | flops 400000000 | bytes 2000000 | tf_op jit(solution)/shard_map/pallas_call | solution.py:675
  86.7 0.7 copy.8
  87.5 0.7 copy.9
Async XLA Ops:
  0.6 0.7 copy-start.3
  1.3 1.0 %copy-start = (bf16[4,2,3,8,8,128]{5,4,3,2,1,0:T(8,128)(2,1)S(1)}, bf16[4,2,3,8,8,128]{5,4,3,2,1,0:T(8,128)(2,1)}, u32[]{:S(2)}) copy-start(bf16[4,2,3,8,8,128]{5,4,3,2,1,0:T(8,128)(2,1)} %param.5) | copy-start | bytes 1179652
  2.3 1.0 %copy-start.1 = (bf16[4,2,3,8,8,128]{5,4,3,2,1,0:T(8,128)(2,1)S(1)}, bf16[4,2,3,8,8,128]{5,4,3,2,1,0:T(8,128)(2,1)}, u32[]{:S(2)}) copy-start(bf16[4,2,3,8,8,128]{5,4,3,2,1,0:T(8,128)(2,1)} %param.6) | copy-start | bytes 1179652
  3.3 0.7 copy-start.2

commit v3 on v2

--- a/solution.py
+++ b/solution.py
@@ -16,7 +16,7 @@
 
 def kernel(
     dims, pos_ref, u_ref, c_ref, m_ref, sol_ref, res_ref,
-    full_c, full_u, ind_all, induct, krylov, work, total, inverse, coef, outer,
+    full_c, full_u, ind_all, induct, krylov, work, total, inverse, coef,
     part, parts, row_out, row_in, col_out, col_in,
     img_row_out, img_row_in, img_col_out, img_col_in, row_r, row_v, col_r, col_v,
     own_sem, gather_send, gather_recv, ind_send, ind_recv, sum_send, sum_recv, halo_send, halo_recv,
@@ -167,6 +167,8 @@
             resid[s, pl.ds(comp * depth, depth)] = real
             resid[s, pl.ds(half + comp * depth, depth)] = 0.5 * real
 
+    base = sources * vecs
+
     def sum_copy(index, count, offset):
         return pltpu.make_async_remote_copy(
             src_ref=part.at[index, pl.ds(0, count)],
@@ -187,27 +189,44 @@
             sum_copy(index, count, offset).wait()
         return jnp.sum(parts[index, :, pl.ds(0, count)], axis=0)
 
-    def images_inner(index, base, field, piece=None):
-        size = tiles if piece is None else 16
-        at = 0 if piece is None else piece * 16
-
-        def body(k, _):
-            vector = full_c[k, pl.ds(at * width_x, size * width_x)]
-            vector = vector.astype(F32).reshape(size, width_x, width_y)
-            for s in range(sources):
-                product = jnp.sum(vector * field[s, pl.ds(at, size)], axis=0)
-                product = jnp.sum(product, axis=0, keepdims=True)
-                place = pl.ds(base + s * vecs + k, 1)
-                if piece:
-                    product = product + part[index, place]
-                part[index, place] = product
-            return 0
-
-        lax.fori_loop(0, vecs, body, 0)
-
-    def inner(index, row, left, right, s):
-        product = jnp.sum(left[s] * right[s], axis=0)
-        part[index, pl.ds(row, 1)] = jnp.sum(product, axis=0, keepdims=True)
+    def products(field, pairs, first, count, sums):
+        def body(j, sums):
+            sums = list(sums)
+            at = pl.ds(pl.multiple_of(j * 16, 16), 16)
+            pair = pl.ds(j * 2, 2)
+            values = [field[s, pair] for s in range(sources)]
+            for k in range(vecs):
+                vector = full_c[k, at].astype(F32).reshape(2, width_x, width_y)
+                for s in range(sources):
+                    sums[s * vecs + k] += jnp.sum(vector * values[s], axis=0)
+            for i, (left, right) in enumerate(pairs):
+                for s in range(sources):
+                    sums[base + s * len(pairs) + i] += jnp.sum(left[s, pair] * right[s, pair], axis=0)
+            return tuple(sums)
+
+        return lax.fori_loop(first, first + count, body, tuple(sums), unroll=2)
+
+    def blank(count):
+        return [jnp.zeros((width_x, width_y), F32)] * count
+
+    def pack_sums(sums):
+        lane = lax.broadcasted_iota(jnp.int32, (width_x, width_y), 1)
+        packed = jnp.zeros((width_x, width_y), F32)
+        for i, value in enumerate(sums):
+            packed = jnp.where(lane == i, jnp.sum(value, axis=1, keepdims=True), packed)
+        return packed
+
+    def unpack_sums(packed, count):
+        row = jnp.sum(packed, axis=0, keepdims=True)
+        size = (count, width_y)
+        mask = lax.broadcasted_iota(jnp.int32, size, 0) == lax.broadcasted_iota(jnp.int32, size, 1)
+        return jnp.sum(jnp.where(mask, row, 0.0), axis=1, keepdims=True)
+
+    def step_sums(index, field, pairs):
+        count = base + sources * len(pairs)
+        part[index, pl.ds(0, 8)] = pack_sums(products(field, pairs, 0, tiles // 2, blank(count)))
+        group_send(index, 8)
+        return unpack_sums(group_sum(index, 8), count)
 
     def spread(value):
         return jnp.broadcast_to(value, (width_x, width_y))
@@ -245,7 +264,7 @@
                 out[s, pair] = totals[s]
             return 0
 
-        lax.fori_loop(0, tiles // 2, body, 0)
+        lax.fori_loop(0, tiles // 2, body, 0, unroll=3)
 
     east, west = gx + 1 < n_gx, gx >= 1
     north, south = gy + 1 < n_gy, gy >= 1
@@ -490,7 +509,7 @@
 
     wide = vecs * 16
     halves = wide // width_y
-    gram_rows = halves * vecs
+    start = blank(base)
     own[0].wait()
     for piece in range(chunks):
         for step in range(1, n_tx - 1):
@@ -501,29 +520,31 @@
             gather_start(1, 1, 0)
         gather_arrive(0, n_tx - 1, piece)
         lax.fori_loop(piece * (chunk // 16), (piece + 1) * (chunk // 16), gram_body, 0)
-        images_inner(0, gram_rows, resid, piece)
+        start = products(resid, [], piece * 8, 8, start)
         if piece + 1 < chunks:
             image_pack(piece)
     same = lax.rem(lax.broadcasted_iota(jnp.int32, (wide, wide), 0), 16) == lax.rem(
         lax.broadcasted_iota(jnp.int32, (wide, wide), 1), 16
     )
     folded = jnp.sum(jnp.where(same, total[...], 0.0).reshape(vecs, 16, wide), axis=1)
+    gram = jnp.zeros((vecs, width_y), F32)
+    lane = lax.broadcasted_iota(jnp.int32, (width_y, width_y), 0)
+    column = lax.broadcasted_iota(jnp.int32, (width_y, width_y), 1)
     for h in range(halves):
-        part[0, pl.ds(h * vecs, vecs)] = folded[:, h * width_y : (h + 1) * width_y]
-    group_send(0, gram_rows + sources * vecs)
+        pick = (lax.div(lane, 16) + h * (width_y // 16) == column).astype(F32)
+        gram = gram + jnp.dot(
+            folded[:, h * width_y : (h + 1) * width_y], pick,
+            precision=lax.Precision.HIGHEST, preferred_element_type=F32,
+        )
+    part[0, pl.ds(0, vecs)] = gram
+    part[0, pl.ds(vecs, 8)] = pack_sums(start)
+    group_send(0, vecs + 8)
     image_pack(chunks - 1)
     for number in range(2, len(links)):
         image_start(number, 0)
-    first_sum = group_sum(0, gram_rows + sources * vecs)
-    gram = jnp.zeros((vecs, vecs), F32)
-    for h in range(halves):
-        lane = lax.broadcasted_iota(jnp.int32, (width_y, vecs), 0)
-        column = lax.broadcasted_iota(jnp.int32, (width_y, vecs), 1)
-        pick = (lax.div(lane, 16) + h * (width_y // 16) == column).astype(F32)
-        gram = gram + jnp.dot(
-            first_sum[h * vecs : (h + 1) * vecs], pick,
-            precision=lax.Precision.HIGHEST, preferred_element_type=F32,
-        )
+    first_sum = group_sum(0, vecs + 8)
+    gram = first_sum[:vecs, :vecs]
+    start = unpack_sums(first_sum[vecs:], base)
     row_id = lax.broadcasted_iota(jnp.int32, (vecs, vecs), 0)
     eye = (row_id == lax.broadcasted_iota(jnp.int32, (vecs, vecs), 1)).astype(F32)
     wide_row = lax.broadcasted_iota(jnp.int32, (vecs, 2 * vecs), 0)
@@ -538,7 +559,6 @@
         flat = jnp.sum(eye * column, axis=0, keepdims=True)
         return answer, jnp.sum(answer * flat, axis=1, keepdims=True)
 
-    start = jnp.sum(first_sum[gram_rows:], axis=1, keepdims=True)
     weights = [solve(start[s * vecs : (s + 1) * vecs])[0] for s in range(sources)]
     one = jnp.ones((1, 1), F32)
     combine(resid, [(resid, [one] * sources)], [-w for w in weights], full_c)
@@ -547,23 +567,15 @@
     combine_halo(row_r, col_r, [(row_in.at[0], col_in.at[0], [one] * sources)])
 
     every = range(sources)
-    base = sources * vecs
     for cycle in range(CYCLES):
         index = 2 * cycle
         apply(resid, row_r, col_r, work)
         exchange_start(index + 1, work)
-        images_inner(index + 1, 0, work)
-        for s in every:
-            inner(index + 1, base + 4 * s, resid, resid, s)
-            inner(index + 1, base + 4 * s + 1, resid, work, s)
-            inner(index + 1, base + 4 * s + 2, work, work, s)
-            part[index + 1, pl.ds(base + 4 * s + 3, 1)] = jnp.zeros((1, width_y), F32)
-        group_send(index + 1, base + 4 * sources)
-        sums = jnp.sum(group_sum(index + 1, base + 4 * sources), axis=1, keepdims=True)
+        sums = step_sums(index + 1, work, [(resid, resid), (resid, work), (work, work)])
         state = []
         for s in every:
             def got(i):
-                return sums[base + 4 * s + i : base + 4 * s + i + 1]
+                return sums[base + 3 * s + i : base + 3 * s + i + 1]
 
             beta = jnp.sqrt(got(0) + EPS)
             scale = 1.0 / beta
@@ -586,14 +598,8 @@
         apply(krylov, row_v, col_v, work)
         if cycle + 1 < CYCLES:
             exchange_start(index + 2, work)
-        images_inner(index + 2, 0, work)
-        for s in every:
-            inner(index + 2, base + 4 * s, resid, work, s)
-            inner(index + 2, base + 4 * s + 1, krylov, work, s)
-            inner(index + 2, base + 4 * s + 2, work, work, s)
-            inner(index + 2, base + 4 * s + 3, krylov, krylov, s)
-        group_send(index + 2, base + 4 * sources)
-        sums = jnp.sum(group_sum(index + 2, base + 4 * sources), axis=1, keepdims=True)
+        pairs = [(resid, work), (krylov, work), (work, work), (krylov, krylov)]
+        sums = step_sums(index + 2, work, pairs)
         in_r, in_v, in_w, in_g, out_r, out_v = [], [], [], [], [], []
         for s in every:
             def got(i):
@@ -666,7 +672,7 @@
     group = n_gx * n_gy
     field = (sources, tiles, width_x, width_y)
     ind_rows = 3 * induction.shape[1] * width_x
-    most = vecs * 16 // width_y * vecs + sources * vecs
+    most = vecs + 8
     sums, halos = 2 * CYCLES + 1, 2 * CYCLES
     dma = pltpu.SemaphoreType.DMA
     vmem = pl.BlockSpec(memory_space=pltpu.VMEM)
@@ -687,7 +693,6 @@
             pltpu.VMEM((vecs * 16, vecs * 16), F32),
             pltpu.VMEM((vecs, vecs), F32),
             pltpu.VMEM((sources, vecs, width_x, width_y), F32),
-            pltpu.VMEM((8, width_y), F32),
             pltpu.VMEM((sums, most, width_y), F32),
             pltpu.VMEM((sums, group, most, width_y), F32),
             pltpu.VMEM((halos, 2, sources * tiles, width_y), F32),
@@ -715,7 +720,7 @@
             dma((2 * chunks + 4,)),
         ],
         compiler_params=pltpu.CompilerParams(
-            collective_id=0, has_side_effects=True, vmem_limit_bytes=48 * 1024 * 1024
+            collective_id=0, has_side_effects=True, vmem_limit_bytes=60 * 1024 * 1024
         ),
         cost_estimate=pl.CostEstimate(flops=400_000_000, bytes_accessed=2_000_000, transcendentals=20_000),
     )(

time: 88.5 us -> 79 us (0.89)
  Pallas kernels: 82.8 us -> 75.5 us
  local copies, waits for them, and re-layouts: 4.84 us -> 2.57 us
    pallas_call x1, Pallas kernels: 82.8 us -> 75.5 us  [on_device(): pl.pallas_call(functools.partial(kernel, dims), out_shape=(jax.ShapeDtype...]
    unnamed x10 -> x4, local copies, waits for them, and re-layouts: 4.84 us -> 2.57 us
where the time goes in v3:
time: 79 us; the launch traced here: 78.8 us
  Pallas kernels  75.5 us (96%)
  local copies, waits for them, and re-layouts  2.57 us (3%)
    pallas_call x1, Pallas kernels, on_device(): pl.pallas_call(functools.partial(kernel, dims), out_shape=(jax.ShapeDtype...  75.5 us
    unnamed x4, local copies, waits for them, and re-layouts  2.57 us

profile of v3, /device:TPU:0, one launch (start us, length us, event | category | flops | bytes accessed | tf_op | source)
XLA Modules:
  0.0 78.8 jit_solution(9996463194653117078)
XLA Ops:
  0.6 75.5 %shard_map.59 = (f32[2,48,8,128]{3,2,1,0:T(8,128)}, f32[2,48,8,128]{3,2,1,0:T(8,128)}) custom-call(s32[2]{0:T(128)} %pos_ref.1, bf16[4,384,128]{2,1,0:T(8,128)(2,1)} %bitcast.7, bf16[4,384,128]{2,1,0:T(8,128)(2,1)} %bitcast.8, bf16[48,128]{1,0:T(8,128)(2,1)} %bitcast.9), custom_call_target="tpu_custom_call" | custom-call | flops 400000000 | bytes 2000000 | tf_op jit(solution)/shard_map/pallas_call | solution.py:681
  76.2 0.0 copy-start
  76.2 1.8 %copy.8 = f32[2,2,3,8,8,128]{5,4,3,2,1,0:T(8,128)} copy(f32[2,2,3,8,8,128]{5,4,3,2,1,0:T(8,128)} %bitcast.6) | data formatting | bytes 786432
  78.0 0.0 copy-done
  78.0 0.7 copy.9
Async XLA Ops:
  76.2 1.8 %copy-start = (f32[2,48,8,128]{3,2,1,0:T(8,128)S(1)}, f32[2,48,8,128]{3,2,1,0:T(8,128)}, u32[]{:S(2)}) copy-start(f32[2,48,8,128]{3,2,1,0:T(8,128)} %get-tuple-element.5) | copy-start | bytes 1179652

commit v4 on v3

--- a/solution.py
+++ b/solution.py
@@ -16,7 +16,7 @@
 
 def kernel(
     dims, pos_ref, u_ref, c_ref, m_ref, sol_ref, res_ref,
-    full_c, full_u, ind_all, induct, krylov, work, total, inverse, coef,
+    full_c, full_u, ind_all, induct, krylov, work, total, inverse, coef, held,
     part, parts, row_out, row_in, col_out, col_in,
     img_row_out, img_row_in, img_col_out, img_col_in, row_r, row_v, col_r, col_v,
     own_sem, gather_send, gather_recv, ind_send, ind_recv, sum_send, sum_recv, halo_send, halo_recv,
@@ -35,7 +35,6 @@
     tiles = rows // width_x
     vecs = full_c.shape[0]
     half = tiles // 2
-    resid = res_ref
     chunk = 16 * width_x
     chunks = rows // chunk
 
@@ -164,8 +163,8 @@
         primary = jnp.exp(-dist / ((size_x + size_y) / 8.0))
         for comp, weight in enumerate((1.0, 0.5, 0.25)):
             real = (induct[comp] - 1.0) * weight * primary
-            resid[s, pl.ds(comp * depth, depth)] = real
-            resid[s, pl.ds(half + comp * depth, depth)] = 0.5 * real
+            res_ref[s, pl.ds(comp * depth, depth)] = real
+            res_ref[s, pl.ds(half + comp * depth, depth)] = 0.5 * real
 
     base = sources * vecs
 
@@ -222,21 +221,21 @@
         mask = lax.broadcasted_iota(jnp.int32, size, 0) == lax.broadcasted_iota(jnp.int32, size, 1)
         return jnp.sum(jnp.where(mask, row, 0.0), axis=1, keepdims=True)
 
-    def step_sums(index, field, pairs):
+    def step_sums(index, field, pairs, meanwhile):
         count = base + sources * len(pairs)
         part[index, pl.ds(0, 8)] = pack_sums(products(field, pairs, 0, tiles // 2, blank(count)))
         group_send(index, 8)
+        meanwhile()
         return unpack_sums(group_sum(index, 8), count)
 
     def spread(value):
         return jnp.broadcast_to(value, (width_x, width_y))
 
-    def combine(out, terms, rows_of, stack, extra=None):
+    def combine(out, terms, rows_of, stack):
         for s in range(sources):
             for k in range(vecs):
                 coef[s, k] = spread(rows_of[s][:, k : k + 1])
         wide = [[spread(c[s]) for s in range(sources)] for _, c in terms]
-        wide_extra = [[spread(c[s]) for s in range(sources)] for _, c in extra[1]] if extra else []
 
         def body(j, _):
             at = pl.ds(pl.multiple_of(j * 16, 16), 16)
@@ -248,14 +247,6 @@
                     now = ref[s, pair] * w[s][None]
                     value = now if value is None else value + now
                 totals.append(value)
-            if extra:
-                out2, terms2, keep = extra
-                for s in range(sources):
-                    value = out2[s, pair] if keep else None
-                    for (ref, _), w in zip(terms2, wide_extra):
-                        now = ref[s, pair] * w[s][None]
-                        value = now if value is None else value + now
-                    out2[s, pair] = value
             for k in range(vecs):
                 vector = stack[k, at, :].astype(F32).reshape(2, width_x, width_y)
                 for s in range(sources):
@@ -265,6 +256,20 @@
             return 0
 
         lax.fori_loop(0, tiles // 2, body, 0, unroll=3)
+
+    def accumulate(cycle, of_r, of_v):
+        wide = [[spread(c[s]) for s in range(sources)] for c in (of_r, of_v)]
+
+        def body(j, _):
+            pair = pl.ds(j * 4, 4)
+            for s in range(sources):
+                value = held[cycle, s, pair] * wide[0][s][None] + krylov[s, pair] * wide[1][s][None]
+                if cycle:
+                    value = value + sol_ref[s, pair]
+                sol_ref[s, pair] = value
+            return 0
+
+        lax.fori_loop(0, tiles // 4, body, 0)
 
     east, west = gx + 1 < n_gx, gx >= 1
     north, south = gy + 1 < n_gy, gy >= 1
@@ -367,7 +372,7 @@
                 img_col_out[side, k] = column
             return 0
 
-        lax.fori_loop(0, vecs, body, 0)
+        lax.fori_loop(0, vecs, body, 0, unroll=4)
         for number in range(2):
             image_start(number, piece)
 
@@ -458,7 +463,7 @@
         def minus_z(f):
             return jnp.concatenate([zero, f[:-1]], axis=0)
 
-        def body(s, _):
+        for s in range(sources):
             for p in range(2):
                 def comp(c):
                     return field[s, pl.ds(p * half + c * depth, depth)]
@@ -467,7 +472,7 @@
                     return s * tiles + p * half + c * depth
 
                 def row(place, c):
-                    return row_halo[place, pl.ds(pl.multiple_of(at(c), 8), depth)]
+                    return row_halo[place, pl.ds(at(c), depth)]
 
                 e_x, e_y, e_z = comp(0), comp(1), comp(2)
                 xp_y = plus_y(e_x, columns(1, at(0)))
@@ -495,11 +500,8 @@
                     cross = induct[number] * field[s, pl.ds((1 - p) * half + number * depth, depth)]
                     value = value - cross if p == 0 else value + cross
                     out[s, pl.ds(p * half + number * depth, depth)] = value
-            return 0
-
-        lax.fori_loop(0, sources, body, 0)
-
-    exchange_start(0, resid)
+
+    exchange_start(0, res_ref)
     total[...] = jnp.zeros_like(total)
 
     def gram_body(j, _):
@@ -520,7 +522,7 @@
             gather_start(1, 1, 0)
         gather_arrive(0, n_tx - 1, piece)
         lax.fori_loop(piece * (chunk // 16), (piece + 1) * (chunk // 16), gram_body, 0)
-        start = products(resid, [], piece * 8, 8, start)
+        start = products(res_ref, [], piece * 8, 8, start)
         if piece + 1 < chunks:
             image_pack(piece)
     same = lax.rem(lax.broadcasted_iota(jnp.int32, (wide, wide), 0), 16) == lax.rem(
@@ -549,9 +551,17 @@
     eye = (row_id == lax.broadcasted_iota(jnp.int32, (vecs, vecs), 1)).astype(F32)
     wide_row = lax.broadcasted_iota(jnp.int32, (vecs, 2 * vecs), 0)
     system = jnp.concatenate([gram, eye], axis=1)
-    for k in range(vecs):
-        pivot = system[k : k + 1] / system[k : k + 1, k : k + 1]
-        system = jnp.where(wide_row == k, pivot, system - system[:, k : k + 1] * pivot)
+    for k in range(0, vecs, 2):
+        col_0 = jnp.broadcast_to(system[:, k : k + 1], (vecs, 2 * vecs))
+        col_1 = jnp.broadcast_to(system[:, k + 1 : k + 2], (vecs, 2 * vecs))
+        top, low = system[k : k + 1], system[k + 1 : k + 2]
+        p_00, p_01 = col_0[k : k + 1], col_1[k : k + 1]
+        p_10, p_11 = col_0[k + 1 : k + 2], col_1[k + 1 : k + 2]
+        scale = 1.0 / (p_00 * p_11 - p_01 * p_10)
+        new_0 = (p_11 * top - p_01 * low) * scale
+        new_1 = (p_00 * low - p_10 * top) * scale
+        system = system - col_0 * new_0 - col_1 * new_1
+        system = jnp.where(wide_row == k, new_0, jnp.where(wide_row == k + 1, new_1, system))
     inverse[...] = system[:, vecs:]
 
     def solve(column):
@@ -561,7 +571,7 @@
 
     weights = [solve(start[s * vecs : (s + 1) * vecs])[0] for s in range(sources)]
     one = jnp.ones((1, 1), F32)
-    combine(resid, [(resid, [one] * sources)], [-w for w in weights], full_c)
+    combine(held.at[0], [(res_ref, [one] * sources)], [-w for w in weights], full_c)
     exchange_wait(0)
     image_wait()
     combine_halo(row_r, col_r, [(row_in.at[0], col_in.at[0], [one] * sources)])
@@ -569,9 +579,15 @@
     every = range(sources)
     for cycle in range(CYCLES):
         index = 2 * cycle
+        resid = held.at[cycle]
         apply(resid, row_r, col_r, work)
-        exchange_start(index + 1, work)
-        sums = step_sums(index + 1, work, [(resid, resid), (resid, work), (work, work)])
+
+        def meanwhile():
+            exchange_start(index + 1, work)
+            if cycle:
+                accumulate(cycle - 1, *update)
+
+        sums = step_sums(index + 1, work, [(resid, resid), (resid, work), (work, work)], meanwhile)
         state = []
         for s in every:
             def got(i):
@@ -596,10 +612,13 @@
         if cycle + 1 < n_tx - 1:
             gather_arrive(1, cycle + 1, 0, True)
         apply(krylov, row_v, col_v, work)
-        if cycle + 1 < CYCLES:
-            exchange_start(index + 2, work)
+
+        def meanwhile():
+            if cycle + 1 < CYCLES:
+                exchange_start(index + 2, work)
+
         pairs = [(resid, work), (krylov, work), (work, work), (krylov, krylov)]
-        sums = step_sums(index + 2, work, pairs)
+        sums = step_sums(index + 2, work, pairs, meanwhile)
         in_r, in_v, in_w, in_g, out_r, out_v = [], [], [], [], [], []
         for s in every:
             def got(i):
@@ -637,8 +656,9 @@
             out_r.append(y_0 * scale)
             out_v.append(y_1)
             weights[s] = weights[s] - (g_0 * y_0 + g_1 * y_1)
-        update = (sol_ref, [(resid, out_r), (krylov, out_v)], cycle > 0)
-        combine(resid, [(resid, in_r), (krylov, in_v), (work, in_w)], in_g, full_c, update)
+        update = (out_r, out_v)
+        target = held.at[cycle + 1] if cycle + 1 < CYCLES else res_ref
+        combine(target, [(resid, in_r), (krylov, in_v), (work, in_w)], in_g, full_c)
         if cycle + 1 < CYCLES:
             exchange_wait(index + 2)
             now = (row_in.at[index + 2], col_in.at[index + 2])
@@ -648,7 +668,10 @@
         gather_arrive(1, step, 0, True)
     gather_arrive(1, n_tx - 1, 0)
     own[1].wait()
-    combine(sol_ref, [(sol_ref, [one] * sources)], weights, full_u)
+    terms = [(held.at[CYCLES - 1], update[0]), (krylov, update[1])]
+    if CYCLES > 1:
+        terms.append((sol_ref, [one] * sources))
+    combine(sol_ref, terms, weights, full_u)
     gather_sent(0)
     gather_sent(1)
     for index in range(2 * CYCLES):
@@ -693,6 +716,7 @@
             pltpu.VMEM((vecs * 16, vecs * 16), F32),
             pltpu.VMEM((vecs, vecs), F32),
             pltpu.VMEM((sources, vecs, width_x, width_y), F32),
+            pltpu.VMEM((CYCLES,) + field, F32),
             pltpu.VMEM((sums, most, width_y), F32),
             pltpu.VMEM((sums, group, most, width_y), F32),
             pltpu.VMEM((halos, 2, sources * tiles, width_y), F32),

time: 79 us -> 75.8 us (0.959)
  Pallas kernels: 75.5 us -> 72.4 us
    pallas_call x1, Pallas kernels: 75.5 us -> 72.4 us  [on_device(): pl.pallas_call(functools.partial(kernel, dims), out_shape=(jax.ShapeDtype...]
where the time goes in v4:
time: 75.8 us; the launch traced here: 75.6 us
  Pallas kernels  72.4 us (96%)
  local copies, waits for them, and re-layouts  2.57 us (3%)
    pallas_call x1, Pallas kernels, on_device(): pl.pallas_call(functools.partial(kernel, dims), out_shape=(jax.ShapeDtype...  72.4 us
    unnamed x4, local copies, waits for them, and re-layouts  2.57 us

profile of v4, /device:TPU:0, one launch (start us, length us, event | category | flops | bytes accessed | tf_op | source)
XLA Modules:
  0.0 75.6 jit_solution(6073850430301218311)
XLA Ops:
  0.6 72.4 %shard_map.59 = (f32[2,48,8,128]{3,2,1,0:T(8,128)}, f32[2,48,8,128]{3,2,1,0:T(8,128)}) custom-call(s32[2]{0:T(128)} %pos_ref.1, bf16[4,384,128]{2,1,0:T(8,128)(2,1)} %bitcast.7, bf16[4,384,128]{2,1,0:T(8,128)(2,1)} %bitcast.8, bf16[48,128]{1,0:T(8,128)(2,1)} %bitcast.9), custom_call_target="tpu_custom_call" | custom-call | flops 400000000 | bytes 2000000 | tf_op jit(solution)/shard_map/pallas_call | solution.py:704
  73.0 0.0 copy-start
  73.0 1.8 %copy.8 = f32[2,2,3,8,8,128]{5,4,3,2,1,0:T(8,128)} copy(f32[2,2,3,8,8,128]{5,4,3,2,1,0:T(8,128)} %bitcast.6) | data formatting | bytes 786432
  74.8 0.0 copy-done
  74.8 0.7 copy.9
Async XLA Ops:
  73.0 1.8 %copy-start = (f32[2,48,8,128]{3,2,1,0:T(8,128)S(1)}, f32[2,48,8,128]{3,2,1,0:T(8,128)}, u32[]{:S(2)}) copy-start(f32[2,48,8,128]{3,2,1,0:T(8,128)} %get-tuple-element.5) | copy-start | bytes 1179652

commit v5 on v4

--- a/solution.py
+++ b/solution.py
@@ -83,32 +83,41 @@
     def receives(way, step):
         return tx - step >= 0 if way == 0 else tx + step < n_tx
 
-    def gather_start(which, step, piece):
+    def forwards(way, step):
+        return sends(way, step + 1)
+
+    def gather_start(which, way, piece, when):
+        @pl.when(jnp.logical_and(sends(way, 1), when))
+        def _():
+            hop(which, way, 1, piece).start()
+
+    def gather_arrive(which, way, step, piece, when):
+        @pl.when(jnp.logical_and(receives(way, step), when))
+        def _():
+            full = (full_c, full_u)[which]
+            at = rows_at(which, piece)
+            shard = tx - step if way == 0 else tx + step
+            pltpu.make_async_remote_copy(
+                src_ref=full.at[slot(shard), at],
+                dst_ref=full.at[slot(shard), at],
+                send_sem=gather_send.at[which, way, step - 1, piece],
+                recv_sem=gather_recv.at[which, way, step - 1, piece],
+                device_id=along(1),
+                device_id_type=MESH,
+            ).wait_recv()
+
+    def gather_forward(which, step, piece):
         for way in range(2):
-            @pl.when(sends(way, step))
+            gather_arrive(which, way, step, piece, forwards(way, step))
+
+            @pl.when(forwards(way, step))
             def _():
-                hop(which, way, step, piece).start()
-
-    def gather_arrive(which, step, piece, then=False):
-        for way in range(2):
-            @pl.when(receives(way, step))
-            def _():
-                full = (full_c, full_u)[which]
-                at = rows_at(which, piece)
-                shard = tx - step if way == 0 else tx + step
-                pltpu.make_async_remote_copy(
-                    src_ref=full.at[slot(shard), at],
-                    dst_ref=full.at[slot(shard), at],
-                    send_sem=gather_send.at[which, way, step - 1, piece],
-                    recv_sem=gather_recv.at[which, way, step - 1, piece],
-                    device_id=along(1),
-                    device_id_type=MESH,
-                ).wait_recv()
-
-            if then:
-                @pl.when(sends(way, step + 1))
-                def _():
-                    hop(which, way, step + 1, piece).start()
+                hop(which, way, step + 1, piece).start()
+
+    def gather_rest(which, piece):
+        for step in range(1, n_tx):
+            for way in range(2):
+                gather_arrive(which, way, step, piece, jnp.logical_not(forwards(way, step)))
 
     def gather_sent(which):
         for piece in range(pieces[which]):
@@ -122,6 +131,7 @@
         pltpu.make_async_copy(ref, full.at[slot(tx)], own_sem.at[number])
         for number, (ref, full) in enumerate(((c_ref, full_c), (u_ref, full_u)))
     ]
+    own.append(pltpu.make_async_copy(m_ref, ind_all.at[tx], own_sem.at[2]))
 
     def ind_copy(offset):
         return pltpu.make_async_remote_copy(
@@ -135,11 +145,14 @@
 
     for offset in range(1, n_tx):
         ind_copy(offset).start()
-    gather_start(0, 1, 0)
-    gather_start(0, 1, 1)
+    for piece in range(chunks):
+        for way in range(2):
+            gather_start(0, way, piece, True)
+    for way in range(2):
+        gather_start(1, way, 0, jnp.logical_not(forwards(way, 1)))
     for copy in own:
         copy.start()
-    ind_all[pl.ds(tx, 1)] = m_ref[...][None]
+    own[2].wait()
     for offset in range(1, n_tx):
         ind_copy(offset).wait()
     layers = depth // n_tx
@@ -515,12 +528,11 @@
     own[0].wait()
     for piece in range(chunks):
         for step in range(1, n_tx - 1):
-            gather_arrive(0, step, piece, True)
-        if piece + 2 < chunks:
-            gather_start(0, 1, piece + 2)
-        elif piece + 1 == chunks:
-            gather_start(1, 1, 0)
-        gather_arrive(0, n_tx - 1, piece)
+            gather_forward(0, step, piece)
+        if piece + 1 == chunks:
+            for way in range(2):
+                gather_start(1, way, 0, forwards(way, 1))
+        gather_rest(0, piece)
         lax.fori_loop(piece * (chunk // 16), (piece + 1) * (chunk // 16), gram_body, 0)
         start = products(res_ref, [], piece * 8, 8, start)
         if piece + 1 < chunks:
@@ -584,6 +596,8 @@
 
         def meanwhile():
             exchange_start(index + 1, work)
+            if index + 1 < n_tx - 1:
+                gather_forward(1, index + 1, 0)
             if cycle:
                 accumulate(cycle - 1, *update)
 
@@ -609,13 +623,13 @@
         exchange_wait(index + 1)
         now = (row_in.at[index + 1], col_in.at[index + 1])
         combine_halo(row_v, col_v, [now + (of_w,), (row_r, col_r, of_r)])
-        if cycle + 1 < n_tx - 1:
-            gather_arrive(1, cycle + 1, 0, True)
         apply(krylov, row_v, col_v, work)
 
         def meanwhile():
             if cycle + 1 < CYCLES:
                 exchange_start(index + 2, work)
+            if index + 2 < n_tx - 1:
+                gather_forward(1, index + 2, 0)
 
         pairs = [(resid, work), (krylov, work), (work, work), (krylov, krylov)]
         sums = step_sums(index + 2, work, pairs, meanwhile)
@@ -664,9 +678,9 @@
             now = (row_in.at[index + 2], col_in.at[index + 2])
             combine_halo(row_r, col_r, [(row_r, col_r, in_r), (row_v, col_v, in_v), now + (in_w,)])
 
-    for step in range(CYCLES + 1, n_tx - 1):
-        gather_arrive(1, step, 0, True)
-    gather_arrive(1, n_tx - 1, 0)
+    for step in range(2 * CYCLES + 1, n_tx - 1):
+        gather_forward(1, step, 0)
+    gather_rest(1, 0)
     own[1].wait()
     terms = [(held.at[CYCLES - 1], update[0]), (krylov, update[1])]
     if CYCLES > 1:
@@ -699,12 +713,12 @@
     sums, halos = 2 * CYCLES + 1, 2 * CYCLES
     dma = pltpu.SemaphoreType.DMA
     vmem = pl.BlockSpec(memory_space=pltpu.VMEM)
-    hbm = pl.BlockSpec(memory_space=pl.ANY)
+    hbm = pl.BlockSpec(memory_space=pltpu.HBM)
     chunks = tiles // 16
     out = pl.pallas_call(
         functools.partial(kernel, dims),
         out_shape=(jax.ShapeDtypeStruct(field, F32),) * 2,
-        in_specs=[pl.BlockSpec(memory_space=pltpu.SMEM), hbm, hbm, vmem],
+        in_specs=[pl.BlockSpec(memory_space=pltpu.SMEM), hbm, hbm, hbm],
         out_specs=(vmem, vmem),
         scratch_shapes=[
             pltpu.VMEM((vecs, rows, width_y), jnp.bfloat16),
@@ -731,7 +745,7 @@
             pltpu.VMEM((2, sources * tiles, width_y), F32),
             pltpu.VMEM((4, width_x, width_y), F32),
             pltpu.VMEM((4, width_x, width_y), F32),
-            dma((2,)),
+            dma((3,)),
             dma((2, 2, n_tx - 1, chunks)),
             dma((2, 2, n_tx - 1, chunks)),
             dma((n_tx - 1,)),
@@ -744,7 +758,7 @@
             dma((2 * chunks + 4,)),
         ],
         compiler_params=pltpu.CompilerParams(
-            collective_id=0, has_side_effects=True, vmem_limit_bytes=60 * 1024 * 1024
+            collective_id=0, has_side_effects=True, vmem_limit_bytes=48 * 1024 * 1024
         ),
         cost_estimate=pl.CostEstimate(flops=400_000_000, bytes_accessed=2_000_000, transcendentals=20_000),
     )(

time: 75.8 us -> 80.1 us (1.057)
  local copies, waits for them, and re-layouts: 2.57 us -> 4.84 us
  Pallas kernels: 72.4 us -> 74.4 us
    unnamed x4 -> x10, local copies, waits for them, and re-layouts: 2.57 us -> 4.84 us
    pallas_call x1, Pallas kernels: 72.4 us -> 74.4 us  [on_device(): pl.pallas_call(functools.partial(kernel, dims), out_shape=(jax.ShapeDtype...]
where the time goes in v5:
time: 80.1 us; the launch traced here: 79.8 us
  Pallas kernels  74.4 us (93%)
  local copies, waits for them, and re-layouts  4.84 us (6%)
    pallas_call x1, Pallas kernels, on_device(): pl.pallas_call(functools.partial(kernel, dims), out_shape=(jax.ShapeDtype...  74.4 us
    unnamed x10, local copies, waits for them, and re-layouts  4.84 us

profile of v5, /device:TPU:0, one launch (start us, length us, event | category | flops | bytes accessed | tf_op | source)
XLA Modules:
  0.0 79.8 jit_solution(160540471529597652)
XLA Ops:
  0.6 0.0 copy-start.3
  0.6 0.6 copy-done.3
  1.3 0.0 copy-start
  1.3 1.0 %copy-done = bf16[4,2,3,8,8,128]{5,4,3,2,1,0:T(8,128)(2,1)S(1)} copy-done((bf16[4,2,3,8,8,128]{5,4,3,2,1,0:T(8,128)(2,1)S(1)}, bf16[4,2,3,8,8,128]{5,4,3,2,1,0:T(8,128)(2,1)}, u32[]{:S(2)}) %copy-start) | copy-done | bytes 393240
  2.3 0.0 copy-start.1
  2.3 1.0 %copy-done.1 = bf16[4,2,3,8,8,128]{5,4,3,2,1,0:T(8,128)(2,1)S(1)} copy-done((bf16[4,2,3,8,8,128]{5,4,3,2,1,0:T(8,128)(2,1)S(1)}, bf16[4,2,3,8,8,128]{5,4,3,2,1,0:T(8,128)(2,1)}, u32[]{:S(2)}) %copy-start.1) | copy-done | bytes 393240
  3.3 0.0 copy-start.2
  3.3 0.7 copy-done.2
  4.0 74.4 %shard_map.59 = (f32[2,48,8,128]{3,2,1,0:T(8,128)S(1)}, f32[2,48,8,128]{3,2,1,0:T(8,128)S(1)}) custom-call(s32[2]{0:T(128)S(1)} %copy-done.3, bf16[4,384,128]{2,1,0:T(8,128)(2,1)S(1)} %bitcast.7, bf16[4,384,128]{2,1,0:T(8,128)(2,1)S(1)} %bitcast.8, bf16[48,128]{1,0:T(8,128)(2,1)S(1)} %bitcast.9), custom_call_target="tpu_custom_call" | custom-call | flops 400000000 | bytes 2000000 | tf_op jit(solution)/shard_map/pallas_call | solution.py:718
  78.3 0.7 copy.8
  79.1 0.7 copy.9
Async XLA Ops:
  0.6 0.7 copy-start.3
  1.3 1.0 %copy-start = (bf16[4,2,3,8,8,128]{5,4,3,2,1,0:T(8,128)(2,1)S(1)}, bf16[4,2,3,8,8,128]{5,4,3,2,1,0:T(8,128)(2,1)}, u32[]{:S(2)}) copy-start(bf16[4,2,3,8,8,128]{5,4,3,2,1,0:T(8,128)(2,1)} %param.5) | copy-start | bytes 1179652
  2.3 1.0 %copy-start.1 = (bf16[4,2,3,8,8,128]{5,4,3,2,1,0:T(8,128)(2,1)S(1)}, bf16[4,2,3,8,8,128]{5,4,3,2,1,0:T(8,128)(2,1)}, u32[]{:S(2)}) copy-start(bf16[4,2,3,8,8,128]{5,4,3,2,1,0:T(8,128)(2,1)} %param.6) | copy-start | bytes 1179652
  3.3 0.7 copy-start.2

commit v6 on v5

--- a/solution.py
+++ b/solution.py
@@ -16,7 +16,7 @@
 
 def kernel(
     dims, pos_ref, u_ref, c_ref, m_ref, sol_ref, res_ref,
-    full_c, full_u, ind_all, induct, krylov, work, total, inverse, coef, held,
+    full_c, full_u, ind_all, induct, krylov, work, total, inverse, coef, held, wide_c,
     part, parts, row_out, row_in, col_out, col_in,
     img_row_out, img_row_in, img_col_out, img_col_in, row_r, row_v, col_r, col_v,
     own_sem, gather_send, gather_recv, ind_send, ind_recv, sum_send, sum_recv, halo_send, halo_recv,
@@ -145,11 +145,9 @@
 
     for offset in range(1, n_tx):
         ind_copy(offset).start()
-    for piece in range(chunks):
+    for piece in range(min(2, chunks)):
         for way in range(2):
             gather_start(0, way, piece, True)
-    for way in range(2):
-        gather_start(1, way, 0, jnp.logical_not(forwards(way, 1)))
     for copy in own:
         copy.start()
     own[2].wait()
@@ -201,14 +199,21 @@
             sum_copy(index, count, offset).wait()
         return jnp.sum(parts[index, :, pl.ds(0, count)], axis=0)
 
+    def widen(piece):
+        def body(k, _):
+            vector = full_c[k, pl.ds(piece * chunk, chunk)].astype(F32)
+            wide_c[k, pl.ds(piece * 16, 16)] = vector.reshape(16, width_x, width_y)
+            return 0
+
+        lax.fori_loop(0, vecs, body, 0, unroll=2)
+
     def products(field, pairs, first, count, sums):
         def body(j, sums):
             sums = list(sums)
-            at = pl.ds(pl.multiple_of(j * 16, 16), 16)
             pair = pl.ds(j * 2, 2)
             values = [field[s, pair] for s in range(sources)]
             for k in range(vecs):
-                vector = full_c[k, at].astype(F32).reshape(2, width_x, width_y)
+                vector = wide_c[k, pair]
                 for s in range(sources):
                     sums[s * vecs + k] += jnp.sum(vector * values[s], axis=0)
             for i, (left, right) in enumerate(pairs):
@@ -244,6 +249,8 @@
     def spread(value):
         return jnp.broadcast_to(value, (width_x, width_y))
 
+    span = 6
+
     def combine(out, terms, rows_of, stack):
         for s in range(sources):
             for k in range(vecs):
@@ -251,8 +258,8 @@
         wide = [[spread(c[s]) for s in range(sources)] for _, c in terms]
 
         def body(j, _):
-            at = pl.ds(pl.multiple_of(j * 16, 16), 16)
-            pair = pl.ds(j * 2, 2)
+            at = pl.ds(pl.multiple_of(j * (span * width_x), 16), span * width_x)
+            pair = pl.ds(j * span, span)
             totals = []
             for s in range(sources):
                 value = None
@@ -261,14 +268,17 @@
                     value = now if value is None else value + now
                 totals.append(value)
             for k in range(vecs):
-                vector = stack[k, at, :].astype(F32).reshape(2, width_x, width_y)
+                if stack is wide_c:
+                    vector = stack[k, pair]
+                else:
+                    vector = stack[k, at].astype(F32).reshape(span, width_x, width_y)
                 for s in range(sources):
                     totals[s] = totals[s] + vector * coef[s, k][None]
             for s in range(sources):
                 out[s, pair] = totals[s]
             return 0
 
-        lax.fori_loop(0, tiles // 2, body, 0, unroll=3)
+        lax.fori_loop(0, tiles // span, body, 0)
 
     def accumulate(cycle, of_r, of_v):
         wide = [[spread(c[s]) for s in range(sources)] for c in (of_r, of_v)]
@@ -376,7 +386,7 @@
             here = jnp.logical_or(here, lane == tile + s * tiles)
 
         def body(k, _):
-            value = full_c[k, pl.ds(piece * chunk, chunk)].astype(F32).reshape(size)
+            value = wide_c[k, pl.ds(piece * 16, 16)]
             for side, (row, col) in enumerate(((0, 0), (width_x - 1, width_y - 1))):
                 img_row_out[side, piece, pl.ds(pl.multiple_of(k * 16, 16), 16)] = value[:, row, :]
                 column = jnp.sum(jnp.where(here, value[:, :, col : col + 1], 0.0), axis=0)
@@ -527,12 +537,19 @@
     start = blank(base)
     own[0].wait()
     for piece in range(chunks):
+        if piece + 1 == chunks:
+            for way in range(2):
+                gather_start(1, way, 0, jnp.logical_not(forwards(way, 1)))
         for step in range(1, n_tx - 1):
             gather_forward(0, step, piece)
+        if piece + 2 < chunks:
+            for way in range(2):
+                gather_start(0, way, piece + 2, True)
         if piece + 1 == chunks:
             for way in range(2):
                 gather_start(1, way, 0, forwards(way, 1))
         gather_rest(0, piece)
+        widen(piece)
         lax.fori_loop(piece * (chunk // 16), (piece + 1) * (chunk // 16), gram_body, 0)
         start = products(res_ref, [], piece * 8, 8, start)
         if piece + 1 < chunks:
@@ -583,7 +600,7 @@
 
     weights = [solve(start[s * vecs : (s + 1) * vecs])[0] for s in range(sources)]
     one = jnp.ones((1, 1), F32)
-    combine(held.at[0], [(res_ref, [one] * sources)], [-w for w in weights], full_c)
+    combine(held.at[0], [(res_ref, [one] * sources)], [-w for w in weights], wide_c)
     exchange_wait(0)
     image_wait()
     combine_halo(row_r, col_r, [(row_in.at[0], col_in.at[0], [one] * sources)])
@@ -619,7 +636,7 @@
             state.append((beta, scale, g_0, n_00, h_00, left, h_10))
         of_w = [v[1] / v[6] for v in state]
         of_r = [-v[4] * v[1] / v[6] for v in state]
-        combine(krylov, [(work, of_w), (resid, of_r)], [-v[2] / v[6] for v in state], full_c)
+        combine(krylov, [(work, of_w), (resid, of_r)], [-v[2] / v[6] for v in state], wide_c)
         exchange_wait(index + 1)
         now = (row_in.at[index + 1], col_in.at[index + 1])
         combine_halo(row_v, col_v, [now + (of_w,), (row_r, col_r, of_r)])
@@ -672,7 +689,7 @@
             weights[s] = weights[s] - (g_0 * y_0 + g_1 * y_1)
         update = (out_r, out_v)
         target = held.at[cycle + 1] if cycle + 1 < CYCLES else res_ref
-        combine(target, [(resid, in_r), (krylov, in_v), (work, in_w)], in_g, full_c)
+        combine(target, [(resid, in_r), (krylov, in_v), (work, in_w)], in_g, wide_c)
         if cycle + 1 < CYCLES:
             exchange_wait(index + 2)
             now = (row_in.at[index + 2], col_in.at[index + 2])
@@ -713,7 +730,7 @@
     sums, halos = 2 * CYCLES + 1, 2 * CYCLES
     dma = pltpu.SemaphoreType.DMA
     vmem = pl.BlockSpec(memory_space=pltpu.VMEM)
-    hbm = pl.BlockSpec(memory_space=pltpu.HBM)
+    hbm = pl.BlockSpec(memory_space=pl.ANY)
     chunks = tiles // 16
     out = pl.pallas_call(
         functools.partial(kernel, dims),
@@ -731,6 +748,7 @@
             pltpu.VMEM((vecs, vecs), F32),
             pltpu.VMEM((sources, vecs, width_x, width_y), F32),
             pltpu.VMEM((CYCLES,) + field, F32),
+            pltpu.VMEM((vecs, tiles, width_x, width_y), F32),
             pltpu.VMEM((sums, most, width_y), F32),
             pltpu.VMEM((sums, group, most, width_y), F32),
             pltpu.VMEM((halos, 2, sources * tiles, width_y), F32),
@@ -758,7 +776,7 @@
             dma((2 * chunks + 4,)),
         ],
         compiler_params=pltpu.CompilerParams(
-            collective_id=0, has_side_effects=True, vmem_limit_bytes=48 * 1024 * 1024
+            collective_id=0, has_side_effects=True, vmem_limit_bytes=60 * 1024 * 1024
         ),
         cost_estimate=pl.CostEstimate(flops=400_000_000, bytes_accessed=2_000_000, transcendentals=20_000),
     )(

time: 80.1 us -> 75.8 us (0.946)
  local copies, waits for them, and re-layouts: 4.84 us -> 2.57 us
  Pallas kernels: 74.4 us -> 72.4 us
    unnamed x10 -> x4, local copies, waits for them, and re-layouts: 4.84 us -> 2.57 us
    pallas_call x1, Pallas kernels: 74.4 us -> 72.4 us  [on_device(): pl.pallas_call(functools.partial(kernel, dims), out_shape=(jax.ShapeDtype...]
where the time goes in v6:
time: 75.8 us; the launch traced here: 75.6 us
  Pallas kernels  72.4 us (96%)
  local copies, waits for them, and re-layouts  2.57 us (3%)
    pallas_call x1, Pallas kernels, on_device(): pl.pallas_call(functools.partial(kernel, dims), out_shape=(jax.ShapeDtype...  72.4 us
    unnamed x4, local copies, waits for them, and re-layouts  2.57 us

profile of v6, /device:TPU:0, one launch (start us, length us, event | category | flops | bytes accessed | tf_op | source)
XLA Modules:
  0.0 75.6 jit_solution(7165953126350610472)
XLA Ops:
  0.6 72.4 %shard_map.59 = (f32[2,48,8,128]{3,2,1,0:T(8,128)}, f32[2,48,8,128]{3,2,1,0:T(8,128)}) custom-call(s32[2]{0:T(128)} %pos_ref.1, bf16[4,384,128]{2,1,0:T(8,128)(2,1)} %bitcast.7, bf16[4,384,128]{2,1,0:T(8,128)(2,1)} %bitcast.8, bf16[48,128]{1,0:T(8,128)(2,1)} %bitcast.9), custom_call_target="tpu_custom_call" | custom-call | flops 400000000 | bytes 2000000 | tf_op jit(solution)/shard_map/pallas_call | solution.py:735
  73.0 0.0 copy-start
  73.0 1.8 %copy.8 = f32[2,2,3,8,8,128]{5,4,3,2,1,0:T(8,128)} copy(f32[2,2,3,8,8,128]{5,4,3,2,1,0:T(8,128)} %bitcast.6) | data formatting | bytes 786432
  74.8 0.0 copy-done
  74.8 0.7 copy.9
Async XLA Ops:
  73.0 1.8 %copy-start = (f32[2,48,8,128]{3,2,1,0:T(8,128)S(1)}, f32[2,48,8,128]{3,2,1,0:T(8,128)}, u32[]{:S(2)}) copy-start(f32[2,48,8,128]{3,2,1,0:T(8,128)} %get-tuple-element.5) | copy-start | bytes 1179652

commit v7 on v6

--- a/solution.py
+++ b/solution.py
@@ -56,9 +56,9 @@
         return pl.ds(shard * per_dev, per_dev)
 
     def rows_at(which, piece):
-        return pl.ds(piece * chunk, chunk) if which == 0 else pl.ds(0, rows)
-
-    pieces = (chunks, 1)
+        return pl.ds(piece * chunk, chunk)
+
+    pieces = (chunks, chunks)
 
     def hop(which, way, step, piece):
         full = (full_c, full_u)[which]
@@ -539,7 +539,7 @@
     for piece in range(chunks):
         if piece + 1 == chunks:
             for way in range(2):
-                gather_start(1, way, 0, jnp.logical_not(forwards(way, 1)))
+                [gather_start(1, way, u, jnp.logical_not(forwards(way, 1))) for u in range(chunks)]
         for step in range(1, n_tx - 1):
             gather_forward(0, step, piece)
         if piece + 2 < chunks:
@@ -547,7 +547,7 @@
                 gather_start(0, way, piece + 2, True)
         if piece + 1 == chunks:
             for way in range(2):
-                gather_start(1, way, 0, forwards(way, 1))
+                [gather_start(1, way, u, forwards(way, 1)) for u in range(chunks)]
         gather_rest(0, piece)
         widen(piece)
         lax.fori_loop(piece * (chunk // 16), (piece + 1) * (chunk // 16), gram_body, 0)
@@ -614,7 +614,7 @@
         def meanwhile():
             exchange_start(index + 1, work)
             if index + 1 < n_tx - 1:
-                gather_forward(1, index + 1, 0)
+                [gather_forward(1, index + 1, u) for u in range(chunks)]
             if cycle:
                 accumulate(cycle - 1, *update)
 
@@ -646,7 +646,7 @@
             if cycle + 1 < CYCLES:
                 exchange_start(index + 2, work)
             if index + 2 < n_tx - 1:
-                gather_forward(1, index + 2, 0)
+                [gather_forward(1, index + 2, u) for u in range(chunks)]
 
         pairs = [(resid, work), (krylov, work), (work, work), (krylov, krylov)]
         sums = step_sums(index + 2, work, pairs, meanwhile)
@@ -696,8 +696,9 @@
             combine_halo(row_r, col_r, [(row_r, col_r, in_r), (row_v, col_v, in_v), now + (in_w,)])
 
     for step in range(2 * CYCLES + 1, n_tx - 1):
-        gather_forward(1, step, 0)
-    gather_rest(1, 0)
+        [gather_forward(1, step, u) for u in range(chunks)]
+    for u in range(chunks):
+        gather_rest(1, u)
     own[1].wait()
     terms = [(held.at[CYCLES - 1], update[0]), (krylov, update[1])]
     if CYCLES > 1:

time: 75.8 us -> 75.8 us (level)
  no operation moved by 1% of the time
where the time goes in v7:
time: 75.8 us; the launch traced here: 75.6 us
  Pallas kernels  72.4 us (96%)
  local copies, waits for them, and re-layouts  2.57 us (3%)
    pallas_call x1, Pallas kernels, on_device(): pl.pallas_call(functools.partial(kernel, dims), out_shape=(jax.ShapeDtype...  72.4 us
    unnamed x4, local copies, waits for them, and re-layouts  2.57 us

profile of v7, /device:TPU:0, one launch (start us, length us, event | category | flops | bytes accessed | tf_op | source)
XLA Modules:
  0.0 75.6 jit_solution(13437805498301706463)
XLA Ops:
  0.6 72.4 %shard_map.59 = (f32[2,48,8,128]{3,2,1,0:T(8,128)}, f32[2,48,8,128]{3,2,1,0:T(8,128)}) custom-call(s32[2]{0:T(128)} %pos_ref.1, bf16[4,384,128]{2,1,0:T(8,128)(2,1)} %bitcast.7, bf16[4,384,128]{2,1,0:T(8,128)(2,1)} %bitcast.8, bf16[48,128]{1,0:T(8,128)(2,1)} %bitcast.9), custom_call_target="tpu_custom_call" | custom-call | flops 400000000 | bytes 2000000 | tf_op jit(solution)/shard_map/pallas_call | solution.py:736
  73.0 0.0 copy-start
  73.0 1.8 %copy.8 = f32[2,2,3,8,8,128]{5,4,3,2,1,0:T(8,128)} copy(f32[2,2,3,8,8,128]{5,4,3,2,1,0:T(8,128)} %bitcast.6) | data formatting | bytes 786432
  74.8 0.0 copy-done
  74.8 0.7 copy.9
Async XLA Ops:
  73.0 1.8 %copy-start = (f32[2,48,8,128]{3,2,1,0:T(8,128)S(1)}, f32[2,48,8,128]{3,2,1,0:T(8,128)}, u32[]{:S(2)}) copy-start(f32[2,48,8,128]{3,2,1,0:T(8,128)} %get-tuple-element.5) | copy-start | bytes 1179652
